TPU v7x, 32 devices: a whole 2x2x4 slice. The times are simulated.
32 devices in a mesh: prow: 4 (over y, x), pcol: 8 (over z, core).
Axes of the slice: x: 2, y: 2, z: 4, core: 2. Of those that a mesh axis runs over, the one named last changes fastest.
Arguments:
- matrix: float32 [16, 4, 256, 8, 8, 256], P(None, 'prow', None, None, 'pcol'), may hold values from -6 to 6
- pivots: int32 [2, 256], replicated, may hold values from 256 to 16383, as said below
- inverse_blocks: float32 [2, 256, 256], replicated, may hold values from -1 to 1
Outputs:
- factored: float32 [16, 4, 256, 8, 8, 256], P(None, 'prow', None, None, 'pcol')
Inputs may be any that keep to these rules, and one draw needn't show every extreme that they name: Entries of pivots[0] lie in 256 to 16383, entries of pivots[1] in 512 to 16383; the entries of one panel are distinct.
All inputs are finite; a program needn't handle non-finite values.
Results may differ from a plain program's by a relative error of at most 0.00013.
Values sent between devices are 32-bit elements; how exact they have to be, the bound alone decides.
No kernel may reach another device: no remote copies, remote signals or barrier semaphores. Data moves between devices by JAX's collectives and lax.ppermute only.
A program may use at most 192 MiB of HBM per device.

v0:
```python
import jax
import jax.numpy as jnp
from jax import lax
from jax.sharding import PartitionSpec as P


def spread(block, axis, source):
    block = jnp.where(lax.axis_index(axis) == source, block, jnp.zeros_like(block))
    return lax.psum(block, axis)


def product(left, right_side):
    return jnp.dot(
        left, right_side, precision=lax.Precision.HIGHEST, preferred_element_type=jnp.float32
    )


def shards(matrix, pivots, inverse_blocks):
    full_shape = matrix.shape
    row_blocks = full_shape[0]
    width = full_shape[2]
    col_blocks = full_shape[3]
    proc_rows = lax.axis_size("prow")
    proc_cols = lax.axis_size("pcol")
    me_row = lax.axis_index("prow")
    me_col = lax.axis_index("pcol")
    local_rows = row_blocks * width
    local_block = matrix.reshape(local_rows, col_blocks * width)
    row_global = jnp.arange(local_rows) // width * proc_rows + me_row
    col_global = jnp.arange(col_blocks * width) // width * proc_cols + me_col
    identity = jnp.eye(width, dtype=jnp.float32)
    for section in range(2):
        root_row = section % proc_rows
        root_col = section % proc_cols
        row_start = section // proc_rows * width
        col_start = section // proc_cols * width
        pivot_list = pivots[section]
        global_block = pivot_list // width
        owned_rows = global_block % proc_rows == me_row
        local_spot = global_block // proc_rows * width + pivot_list % width
        picked = jnp.where(owned_rows[:, None], local_block[local_spot], 0.0)
        current = local_block[row_start : row_start + width]
        pivot_rows = lax.psum(picked, "prow")
        old_rows = spread(current, "prow", root_row)
        local_block = local_block.at[row_start : row_start + width].set(
            jnp.where(me_row == root_row, pivot_rows, current)
        )
        target = jnp.where(owned_rows, local_spot, local_rows)
        local_block = local_block.at[target].set(old_rows, mode="drop")
        packed = inverse_blocks[section]
        upper_inv = jnp.triu(packed)
        lower_inv = jnp.tril(packed, -1) + identity
        column = spread(local_block[:, col_start : col_start + width], "pcol", root_col)
        below_rows = row_global > section
        lower_panel = jnp.where(below_rows[:, None], product(column, upper_inv), 0.0)
        right_cols = col_global > section
        upper_rows = spread(
            product(lower_inv, local_block[row_start : row_start + width]), "prow", root_row
        )
        upper_rows = jnp.where(right_cols[None, :], upper_rows, 0.0)
        local_block = local_block - product(lower_panel, upper_rows)
        new_column = jnp.where(below_rows[:, None], lower_panel, column)
        old_column = local_block[:, col_start : col_start + width]
        local_block = local_block.at[:, col_start : col_start + width].set(
            jnp.where(me_col == root_col, new_column, old_column)
        )
        current = local_block[row_start : row_start + width]
        solved = jnp.where(right_cols[None, :], upper_rows, current)
        local_block = local_block.at[row_start : row_start + width].set(
            jnp.where(me_row == root_row, solved, current)
        )
    return local_block.reshape(full_shape)


def solution(mesh):
    return jax.shard_map(
        shards,
        mesh=mesh,
        in_specs=(P(None, "prow", None, None, "pcol", None), P(), P()),
        out_specs=P(None, "prow", None, None, "pcol", None),
        check_vma=False,
    )
```

profile of v0, /device:TPU:0, one launch (start us, length us, event | category | flops | bytes accessed | tf_op | source)
XLA Modules:
  0.0 937.0 jit_solution(12440142318327129250)
XLA Ops:
  8.1 8.3 slice_reduce_fusion
  16.5 94.1 %reduce.17 = f32[16,256,8,256]{3,2,1,0:T(8,128)} reduce(f32[16,1,256,8,1,256]{5,4,3,2,1,0:T(1,128)} %param.15, f32[]{:T(128)} %constant.271), dimensions={1,4}, to_apply=%param.15.reduce_sub_computation | reduce | bytes 67108864 | tf_op args[0]
  110.5 29.9 %copy.6 = f32[512,8,8,256]{3,1,2,0:T(8,128)} copy(f32[512,8,8,256]{3,2,1,0:T(8,128)} %bitcast.55) | data formatting | bytes 67108864
  143.0 14.1 %gather_fusion = f32[256,2048]{1,0:T(8,128)} fusion(f32[4096,2048]{1,0:T(8,128)} %bitcast.53, s32[1024]{0:T(1024)S(1)} %pad_clamp_fusion.1), kind=kCustom, calls=%fused_computation | custom fusion | bytes 4195328 | tf_op jit(solution)/shard_map/gather | solution.py:41
  161.8 107.0 %all-reduce.19.cloned.1.call-done = (f32[256,2048]{1,0:T(8,128)}, f32[256,2048]{1,0:T(8,128)}) async-done(((f32[256,2048]{1,0:T(8,128)}, f32[256,2048]{1,0:T(8,128)}), (f32[256,2048]{1,0:T(8,128)}, f32[256,2048]{1,0:T(8,128)})) %all-reduce.19.cloned.1.call-update) | async-done | bytes 4194320 | tf_op jit(solution)/shard_map/psum | solution.py:43
  271.9 24.4 %scatter_fusion = f32[4096,2048]{1,0:T(8,128)} fusion(f32[4096,2048]{1,0:T(8,128)} %select_dynamic-update-slice_fusion.1, s32[256]{0:T(256)S(1)} %bitcast.60, f32[256,2048]{1,0:T(8,128)} %get-tuple-element.80), kind=kCustom, calls=%fused_computation.2 | custom fusion | bytes 6292480 | tf_op jit(solution)/shard_map/scatter | solution.py:49
  296.4 4.5 slice_select_fusion.1
  301.9 4.8 convolution_select_fusion.3
  307.8 88.8 %all-reduce.9.cloned.1.call-done = f32[4096,256]{1,0:T(8,128)} async-done(((f32[4096,256]{1,0:T(8,128)}), f32[4096,256]{1,0:T(8,128)}) %all-reduce.9.cloned.1.call-update) | async-done | bytes 4194320 | tf_op jit(solution)/shard_map/psum | solution.py:9
  396.6 6.7 convolution_select_fusion.1
  403.3 66.5 %all-reduce.11.cloned.1.call-done = f32[256,2048]{1,0:T(8,128)} async-done(((f32[256,2048]{1,0:T(8,128)}), f32[256,2048]{1,0:T(8,128)}) %all-reduce.11.cloned.1.call-update) | async-done | bytes 2097168 | tf_op jit(solution)/shard_map/psum | solution.py:9
  469.8 35.1 %convolution_subtract_fusion.1 = f32[4096,2048]{1,0:T(8,128)} fusion(f32[4096,2048]{1,0:T(8,128)} %scatter_fusion, f32[4096,256]{1,0:T(8,128)} %convolution_select_fusion.1, f32[256,2048]{1,0:T(8,128)} %all-reduce.11.cloned.1.call-done, pred[2048]{0:T(1024)(128)(4,1)S(1)} %fusion.35), kind=kOutput, calls=%fused_computation.5 | convolution fusion | flops 25778716672 | bytes 73402368 | tf_op jit(solution)/shard_map/dot_general | solution.py:13
  504.9 4.7 fusion
  514.6 14.2 %gather_fusion.1 = f32[256,2048]{1,0:T(8,128)} fusion(f32[4096,2048]{1,0:T(8,128)} %constant_dynamic-update-slice_fusion, s32[1024]{0:T(1024)S(1)} %pad_clamp_fusion), kind=kCustom, calls=%fused_computation.1 | custom fusion | bytes 4195328 | tf_op jit(solution)/shard_map/gather | solution.py:41
  532.1 104.1 %all-reduce.17.cloned.1.call-done = (f32[256,2048]{1,0:T(8,128)}, f32[256,2048]{1,0:T(8,128)}) async-done(((f32[256,2048]{1,0:T(8,128)}, f32[256,2048]{1,0:T(8,128)}), (f32[256,2048]{1,0:T(8,128)}, f32[256,2048]{1,0:T(8,128)})) %all-reduce.17.cloned.1.call-update) | async-done | bytes 4194320 | tf_op jit(solution)/shard_map/psum | solution.py:43
  637.8 25.1 %scatter_fusion.1 = f32[4096,2048]{1,0:T(8,128)} fusion(f32[4096,2048]{1,0:T(8,128)} %select_dynamic-update-slice_fusion, s32[256]{0:T(256)S(1)} %bitcast.59, f32[256,2048]{1,0:T(8,128)} %get-tuple-element.78), kind=kCustom, calls=%fused_computation.3 | custom fusion | bytes 6292480 | tf_op jit(solution)/shard_map/scatter | solution.py:49
  662.9 4.4 slice_select_fusion
  667.4 4.8 convolution_select_fusion.2
  672.2 93.3 %all-reduce.13.cloned.1.call-done = f32[4096,256]{1,0:T(8,128)} async-done(((f32[4096,256]{1,0:T(8,128)}), f32[4096,256]{1,0:T(8,128)}) %all-reduce.13.cloned.1.call-update) | async-done | bytes 4194320 | tf_op jit(solution)/shard_map/psum | solution.py:9
  765.6 6.7 convolution_select_fusion
  772.3 66.3 %all-reduce.15.cloned.1.call-done = f32[256,2048]{1,0:T(8,128)} async-done(((f32[256,2048]{1,0:T(8,128)}), f32[256,2048]{1,0:T(8,128)}) %all-reduce.15.cloned.1.call-update) | async-done | bytes 2097168 | tf_op jit(solution)/shard_map/psum | solution.py:9
  838.6 34.9 %convolution_subtract_fusion = f32[4096,2048]{1,0:T(8,128)} fusion(f32[4096,2048]{1,0:T(8,128)} %scatter_fusion.1, f32[4096,256]{1,0:T(8,128)} %convolution_select_fusion, f32[256,2048]{1,0:T(8,128)} %all-reduce.15.cloned.1.call-done, pred[2048]{0:T(1024)(128)(4,1)S(1)} %fusion.34), kind=kOutput, calls=%fused_computation.4 | convolution fusion | flops 25778716672 | bytes 73402368 | tf_op jit(solution)/shard_map/dot_general | solution.py:13
  873.5 4.7 fusion.1
  881.6 48.3 %reshape.648 = f32[16,1,256,8,1,256]{5,4,3,2,1,0:T(1,128)} reshape(f32[4096,2048]{1,0:T(8,128)} %fusion.2) | data formatting | bytes 67108864 | tf_op jit(solution)/shard_map/reshape | solution.py:72
  (50 shorter events, 27.5 us)
Async XLA Ops:
  6.5 262.2 %all-reduce.19.cloned.1.call-start = ((), (), s32[]{:S(2)}) async-start(), calls=%async_computation.5 | async-start | bytes 8388608 | tf_op jit(solution)/shard_map/psum | solution.py:43
  161.7 234.9 %all-reduce.9.cloned.1.call-start = ((), (), s32[]{:S(2)}) async-start(), calls=%async_computation | async-start | bytes 8388608 | tf_op jit(solution)/shard_map/psum | solution.py:9
  300.9 1.0 copy-start.6
  300.9 168.9 %all-reduce.11.cloned.1.call-start = ((), (), s32[]{:S(2)}) async-start(), calls=%async_computation.1 | async-start | bytes 4194304 | tf_op jit(solution)/shard_map/psum | solution.py:9
  306.7 329.5 %all-reduce.17.cloned.1.call-start = ((), (), s32[]{:S(2)}) async-start(), calls=%async_computation.4 | async-start | bytes 8388608 | tf_op jit(solution)/shard_map/psum | solution.py:43
  469.8 35.1 %copy-start.1 = (f32[4096,256]{1,0:T(8,128)S(1)}, f32[4096,256]{1,0:T(8,128)}, u32[]{:S(2)}) copy-start(f32[4096,256]{1,0:T(8,128)} %convolution_select_fusion.1) | copy-start | bytes 12582916
  469.8 35.1 %copy-start.2 = (f32[4096,256]{1,0:T(8,128)S(1)}, f32[4096,256]{1,0:T(8,128)}, u32[]{:S(2)}) copy-start(f32[4096,256]{1,0:T(8,128)} %all-reduce.9.cloned.1.call-done) | copy-start | bytes 12582916
  504.9 4.7 copy-start.4
  531.9 233.7 %all-reduce.13.cloned.1.call-start = ((), (), s32[]{:S(2)}) async-start(), calls=%async_computation.2 | async-start | bytes 8388608 | tf_op jit(solution)/shard_map/psum | solution.py:9
  667.3 171.3 %all-reduce.15.cloned.1.call-start = ((), (), s32[]{:S(2)}) async-start(), calls=%async_computation.3 | async-start | bytes 4194304 | tf_op jit(solution)/shard_map/psum | solution.py:9
  838.6 34.9 %copy-start = (f32[4096,256]{1,0:T(8,128)S(1)}, f32[4096,256]{1,0:T(8,128)}, u32[]{:S(2)}) copy-start(f32[4096,256]{1,0:T(8,128)} %convolution_select_fusion) | copy-start | bytes 12582916
  838.6 34.9 %copy-start.3 = (f32[4096,256]{1,0:T(8,128)S(1)}, f32[4096,256]{1,0:T(8,128)}, u32[]{:S(2)}) copy-start(f32[4096,256]{1,0:T(8,128)} %all-reduce.13.cloned.1.call-done) | copy-start | bytes 12582916
  873.5 4.7 copy-start.5
Sparse Core Ops, SparseCore 0:
  161.8 106.8 all-reduce.18
  301.0 95.5 all-reduce.8
  400.0 69.6 all-reduce.10
  532.0 104.1 all-reduce.16
  667.4 98.0 all-reduce.12
  768.8 69.6 all-reduce.14
where the time goes:
time: 945 us; the launch traced here: 937 us
  waiting for transfers between devices  526 us (56%)
  local copies, waits for them, and re-layouts  170 us (18%)
  other arithmetic  134 us (14%)
  matrix products  93.1 us (10%)
  between operations  13.8 us (1%)
    psum x4, waiting for transfers between devices, spread(): return lax.psum(block, axis)  315 us
    psum x2, waiting for transfers between devices, shards(): pivot_rows = lax.psum(picked, 'prow')  211 us
    unnamed x1, other arithmetic  94.1 us
    dot_general x6, matrix products, product(): jnp.dot(left, right_side, precision=lax.Precision.HIGHEST, preferred_elem...  93.1 us
    scatter x2, local copies, waits for them, and re-layouts, shards(): local_block = local_block.at[target].set(old_rows, mode='drop')  49.5 us
    reshape x1, local copies, waits for them, and re-layouts, shards(): return local_block.reshape(full_shape)  48.3 us
    unnamed x16, local copies, waits for them, and re-layouts  33.4 us
    gather x2, local copies, waits for them, and re-layouts, shards(): picked = jnp.where(owned_rows[:, None], local_block[local_spot], 0.0)  28.3 us
  transfers between devices with their start and end apart: 6, of which 6 were waited for; matrix products, arithmetic and copies ran while one was open for 3% of the time, Pallas kernels for 0%

commit v1 on v0

v1 whole, which is shorter than its diff:
```python
import functools

import jax
import jax.numpy as jnp
from jax import lax
from jax.experimental import pallas as pl
from jax.experimental.pallas import tpu as pltpu
from jax.sharding import PartitionSpec as P

LANES = 128
CHUNKS = 8
TILE = 256
F32 = jnp.float32
BF16 = jnp.bfloat16
ANY = pl.BlockSpec(memory_space=pl.ANY)
VMEM = pl.BlockSpec(memory_space=pltpu.VMEM)
SMEM = pl.BlockSpec(memory_space=pltpu.SMEM)
PARAMS = pltpu.CompilerParams(vmem_limit_bytes=56 << 20)


def cost(flops, nbytes):
    return pl.CostEstimate(flops=int(flops), bytes_accessed=int(nbytes), transcendentals=0)


def split(x):
    high = x.astype(BF16)
    return high, (x - high.astype(F32)).astype(BF16)


def dot3(left, right):
    out = jnp.dot(left[0], right[0], preferred_element_type=F32)
    out += jnp.dot(left[0], right[1], preferred_element_type=F32)
    return out + jnp.dot(left[1], right[0], preferred_element_type=F32)


def upper(packed):
    row = lax.broadcasted_iota(jnp.int32, packed.shape, 0)
    col = lax.broadcasted_iota(jnp.int32, packed.shape, 1)
    return jnp.where(col >= row, packed, 0.0)


def unit_lower(packed):
    row = lax.broadcasted_iota(jnp.int32, packed.shape, 0)
    col = lax.broadcasted_iota(jnp.int32, packed.shape, 1)
    return jnp.where(col < row, packed, jnp.where(col == row, 1.0, 0.0))


def get_block(ref, start, count, groups, block, per):
    parts = [
        ref[pl.ds(start * groups + block * per + h, count, stride=groups), :] for h in range(per)
    ]
    return jnp.concatenate(parts, axis=1)


def put_block(ref, start, count, groups, block, per, value):
    for h in range(per):
        ref[pl.ds(start * groups + block * per + h, count, stride=groups), :] = value[
            :, h * LANES : (h + 1) * LANES
        ]


def update_rows(count, groups, per, mc, c0, c1, inv_ref, u01_ref, uhl_ref, m_ref, o_ref):
    width = per * LANES
    l0 = dot3(split(c0), split(upper(inv_ref[0])))
    l0s = split(l0)
    rest = c1 - dot3(l0s, split(u01_ref[...]))
    l1 = dot3(split(rest), split(upper(inv_ref[1])))
    l1s = split(l1)
    high = jnp.concatenate([l0s[0], l1s[0]], axis=1)
    low = jnp.concatenate([l0s[1], l1s[1]], axis=1)
    for block in range(groups // per):
        cols = slice(block * width, (block + 1) * width)
        acc = dot3((high, low), (uhl_ref[0, :, cols], uhl_ref[1, :, cols]))
        new = get_block(m_ref, 0, count, groups, block, per) - acc
        if block == 0:
            new = jnp.where(mc == 0, l0, jnp.where(mc == 1, l1, new))
        put_block(o_ref, 0, count, groups, block, per, new)


def rows_kernel(list_ref, m_ref, o_ref, sem):
    count = o_ref.shape[0]

    def step(k, carry):
        pltpu.make_async_copy(m_ref.at[list_ref[k]], o_ref.at[k], sem).start()
        return carry

    lax.fori_loop(0, count, step, 0)
    pltpu.make_async_copy(o_ref, o_ref, sem).wait()


def take_rows(indices, m4):
    count = indices.shape[0]
    shape = (count,) + m4.shape[1:]
    return pl.pallas_call(
        rows_kernel,
        in_specs=[SMEM, ANY],
        out_specs=ANY,
        out_shape=jax.ShapeDtypeStruct(shape, F32),
        scratch_shapes=[pltpu.SemaphoreType.DMA],
        cost_estimate=cost(0, 4 * shape[0] * shape[1] * shape[2] * shape[3]),
        name="take_rows",
    )(indices, m4)


def send_rows_kernel(info_ref, list_ref, m_ref, *rest):
    outs, sem = rest[:-1], rest[-1]
    count = outs[0].shape[0]

    @pl.when(info_ref[0] < 2)
    def _():
        for x, out in enumerate(outs):

            def step(k, carry):
                pltpu.make_async_copy(m_ref.at[list_ref[x, k]], out.at[k], sem).start()
                return carry

            lax.fori_loop(0, count, step, 0)
        for out in outs:
            pltpu.make_async_copy(out, out, sem).wait()


def send_rows(info, lists, m4):
    kinds, count = lists.shape
    shape = (count,) + m4.shape[1:]
    return pl.pallas_call(
        send_rows_kernel,
        in_specs=[SMEM, SMEM, ANY],
        out_specs=[ANY] * kinds,
        out_shape=[jax.ShapeDtypeStruct(shape, F32)] * kinds,
        scratch_shapes=[pltpu.SemaphoreType.DMA],
        cost_estimate=cost(0, 8 * kinds * shape[0] * shape[1] * shape[2] * shape[3]),
        name="send_rows",
    )(info, lists, m4)


def pick_kernel(first, rows, info_ref, m_ref, recv_ref, o_ref, sem):
    @pl.when(info_ref[2] == 0)
    def _():
        copy = pltpu.make_async_copy(m_ref.at[pl.ds(first, rows), 0], o_ref, sem)
        copy.start()
        copy.wait()

    @pl.when(info_ref[2] != 0)
    def _():
        copy = pltpu.make_async_copy(recv_ref, o_ref, sem)
        copy.start()
        copy.wait()


def pick(info, m4, recv, first):
    return pl.pallas_call(
        functools.partial(pick_kernel, first, recv.shape[0]),
        in_specs=[SMEM, ANY, ANY],
        out_specs=ANY,
        out_shape=jax.ShapeDtypeStruct(recv.shape, F32),
        scratch_shapes=[pltpu.SemaphoreType.DMA],
        cost_estimate=cost(0, 8 * recv.size),
        name="pick",
    )(info, m4, recv)


def panel_kernel(first, rows, m_ref, o_ref, sem):
    copy = pltpu.make_async_copy(m_ref.at[pl.ds(first, rows), 0], o_ref, sem)
    copy.start()
    copy.wait()


def panel(m4, first, rows):
    shape = (rows,) + m4.shape[2:]
    return pl.pallas_call(
        functools.partial(panel_kernel, first, rows),
        in_specs=[ANY],
        out_specs=ANY,
        out_shape=jax.ShapeDtypeStruct(shape, F32),
        scratch_shapes=[pltpu.SemaphoreType.DMA],
        cost_estimate=cost(0, 8 * rows * shape[1] * shape[2]),
        name="panel",
    )(m4)


def assemble_kernel(width, info_ref, index_ref, g_ref, o_ref, tab_ref):
    per = tab_ref.shape[1]
    base = jnp.where(info_ref[3] == 0, width, 0)

    def step(k, carry):
        o_ref[k] = g_ref[index_ref[k]]
        return carry

    def tab_step(k, carry):
        tab_ref[k] = g_ref[index_ref[base + k], 0:per, :]
        return carry

    lax.fori_loop(0, 2 * width, step, 0, unroll=4)
    lax.fori_loop(0, width, tab_step, 0, unroll=4)


def assemble(info, index, gathered, width, per):
    groups = gathered.shape[1]
    return pl.pallas_call(
        functools.partial(assemble_kernel, width),
        in_specs=[SMEM, SMEM, VMEM],
        out_specs=[VMEM, VMEM],
        out_shape=[
            jax.ShapeDtypeStruct((2 * width, groups, LANES), F32),
            jax.ShapeDtypeStruct((width, per, LANES), F32),
        ],
        compiler_params=PARAMS,
        cost_estimate=cost(0, 8 * gathered.size),
        name="assemble",
    )(info, index, gathered)


def fetch_kernel(info_ref, *rest):
    *ins, f_ref, tab_ref, sem = rest
    me = info_ref[0]
    rows = ins[0].shape[0]
    for source in range(2):
        spot = pl.ds(source * rows, rows)
        for x, buf in enumerate(ins):

            @pl.when((me ^ source) == x)
            def _():
                whole = pltpu.make_async_copy(buf, f_ref.at[spot], sem.at[0])
                head = pltpu.make_async_copy(buf.at[:, 0], tab_ref.at[spot], sem.at[1])
                whole.start()
                head.start()
                whole.wait()
                head.wait()


def fetch(info, bufs):
    rows, blocks, per, _ = bufs[0].shape
    return pl.pallas_call(
        fetch_kernel,
        in_specs=[SMEM] + [ANY] * len(bufs),
        out_specs=[ANY, ANY],
        out_shape=[
            jax.ShapeDtypeStruct((2 * rows, blocks, per, LANES), F32),
            jax.ShapeDtypeStruct((2 * rows, per, LANES), F32),
        ],
        scratch_shapes=[pltpu.SemaphoreType.DMA((2,))],
        cost_estimate=cost(0, 16 * bufs[0].size),
        name="fetch",
    )(info, *bufs)


def solve_kernel(groups, per, info_ref, a_ref, own_ref, sib_ref, inv_ref, uhl_ref, brow_ref, u01_ref):
    width = per * LANES
    mc = info_ref[1]
    even = info_ref[3] == 0
    own = get_block(own_ref, 0, width, per, 0, per)
    sib = get_block(sib_ref, 0, width, per, 0, per)
    z1c0 = jnp.where(even, own, sib)
    g0c1 = jnp.where(even, sib, own)
    low0 = split(unit_lower(inv_ref[0]))
    low1 = split(unit_lower(inv_ref[1]))
    l01 = dot3(split(z1c0), split(upper(inv_ref[0])))
    l01s = split(l01)
    u01_ref[...] = dot3(low0, split(g0c1))
    for block in range(groups // per):
        cols = slice(block * width, (block + 1) * width)
        g0 = get_block(a_ref, 0, width, groups, block, per)
        z1 = get_block(a_ref, width, width, groups, block, per)
        u0 = dot3(low0, split(g0))
        u0s = split(u0)
        a1 = z1 - dot3(l01s, u0s)
        u1 = dot3(low1, split(a1))
        u1s = split(u1)
        for part in range(2):
            uhl_ref[part, :width, cols] = u0s[part]
            uhl_ref[part, width:, cols] = u1s[part]
        if block == 0:
            top = jnp.where(mc == 0, g0, u0)
            mid = jnp.where(mc == 0, l01, jnp.where(mc == 1, a1, u1))
        else:
            top, mid = u0, u1
        put_block(brow_ref, 0, width, groups, block, per, top)
        put_block(brow_ref, width, width, groups, block, per, mid)


def solve(info, asm, own, sib, inv, groups, per):
    width = per * LANES
    cols = groups * LANES
    return pl.pallas_call(
        functools.partial(solve_kernel, groups, per),
        in_specs=[SMEM, VMEM, VMEM, VMEM, VMEM],
        out_specs=[VMEM, VMEM, VMEM],
        out_shape=[
            jax.ShapeDtypeStruct((2, 2 * width, cols), BF16),
            jax.ShapeDtypeStruct((2 * width * groups, LANES), F32),
            jax.ShapeDtypeStruct((width, width), F32),
        ],
        compiler_params=PARAMS,
        cost_estimate=cost(18 * width * width * cols, 24 * width * cols),
        name="solve",
    )(info, asm, own, sib, inv)


def bulk_kernel(chips, groups, per, tile, fresh, info_ref, *rest):
    owns, sibs = rest[:chips], rest[chips : 2 * chips]
    m_ref, inv_ref, u01_ref, uhl_ref = rest[2 * chips : 2 * chips + 4]
    o_ref, c0_ref, c1_ref, sem = rest[-4:]
    step = pl.program_id(0)

    @pl.when(step == 0)
    def _():
        for h in range(chips):
            for core in range(2):

                @pl.when((info_ref[2] == h) & (info_ref[3] == core))
                def _():
                    first, second = (owns[h], sibs[h]) if core == 0 else (sibs[h], owns[h])
                    one = pltpu.make_async_copy(first, c0_ref, sem.at[0])
                    two = pltpu.make_async_copy(second, c1_ref, sem.at[1])
                    one.start()
                    two.start()
                    one.wait()
                    two.wait()

    c0 = get_block(c0_ref, step * tile, tile, per, 0, per)
    c1 = get_block(c1_ref, step * tile, tile, per, 0, per)
    update_rows(
        tile, groups, per, info_ref[1], c0, c1, inv_ref, u01_ref, uhl_ref, m_ref, o_ref
    )


def bulk(info, owns, sibs, m2, inv, u01, uhl, out, first, rows, groups, per):
    chips = len(owns)
    tile = min(TILE, rows)
    base = first // tile
    width = per * LANES
    cols = groups * LANES
    block = pl.BlockSpec((tile * groups, LANES), lambda i: (base + i, 0))
    fresh = out is None
    in_specs = [SMEM] + [ANY] * (2 * chips) + [block, VMEM, VMEM, VMEM]
    args = [info, *owns, *sibs, m2, inv, u01, uhl]
    aliases = {}
    if not fresh:
        in_specs.append(ANY)
        aliases = {len(args): 0}
        args.append(out)
    return pl.pallas_call(
        functools.partial(bulk_kernel, chips, groups, per, tile, fresh),
        grid=(rows // tile,),
        in_specs=in_specs,
        out_specs=block,
        out_shape=jax.ShapeDtypeStruct(m2.shape, F32),
        scratch_shapes=[
            pltpu.VMEM((rows * per, LANES), F32),
            pltpu.VMEM((rows * per, LANES), F32),
            pltpu.SemaphoreType.DMA((2,)),
        ],
        input_output_aliases=aliases,
        compiler_params=PARAMS,
        cost_estimate=cost(12 * rows * width * cols, 8 * rows * cols),
        name="bulk",
    )(*args)


def moved_kernel(groups, per, info_ref, f_ref, own_ref, sib_ref, inv_ref, u01_ref, uhl_ref, o_ref):
    rows = f_ref.shape[0] // groups
    even = info_ref[3] == 0
    own = get_block(own_ref, 0, rows, per, 0, per)
    sib = get_block(sib_ref, 0, rows, per, 0, per)
    c0 = jnp.where(even, own, sib)
    c1 = jnp.where(even, sib, own)
    update_rows(rows, groups, per, info_ref[1], c0, c1, inv_ref, u01_ref, uhl_ref, f_ref, o_ref)


def moved(info, f2, own, sib, inv, u01, uhl, groups, per):
    rows = f2.shape[0] // groups
    return pl.pallas_call(
        functools.partial(moved_kernel, groups, per),
        in_specs=[SMEM] + [VMEM] * 6,
        out_specs=VMEM,
        out_shape=jax.ShapeDtypeStruct(f2.shape, F32),
        compiler_params=PARAMS,
        cost_estimate=cost(12 * rows * per * groups * LANES * LANES, 8 * f2.size),
        name="moved",
    )(info, f2, own, sib, inv, u01, uhl)


def place_kernel(info_ref, spot_ref, f_ref, brow_ref, _, o_ref, sem):
    width = brow_ref.shape[0] // 2
    count = f_ref.shape[0]

    def put(k):
        return pltpu.make_async_copy(f_ref.at[k], o_ref.at[spot_ref[k]], sem.at[0])

    def start(k, carry):
        @pl.when(spot_ref[k] >= 0)
        def _():
            put(k).start()

        return carry

    def finish(k, carry):
        @pl.when(spot_ref[k] >= 0)
        def _():
            put(k).wait()

        return carry

    for source in range(2):

        @pl.when(info_ref[0] == source)
        def _():
            pltpu.make_async_copy(
                brow_ref.at[pl.ds(source * width, width)], o_ref.at[pl.ds(0, width)], sem.at[1]
            ).start()

    lax.fori_loop(0, count, start, 0)
    lax.fori_loop(0, count, finish, 0)
    for source in range(2):

        @pl.when(info_ref[0] == source)
        def _():
            pltpu.make_async_copy(
                brow_ref.at[pl.ds(source * width, width)], o_ref.at[pl.ds(0, width)], sem.at[1]
            ).wait()


def place(info, spots, f3, brow, out):
    return pl.pallas_call(
        place_kernel,
        in_specs=[SMEM, SMEM, ANY, ANY, ANY],
        out_specs=ANY,
        out_shape=jax.ShapeDtypeStruct(out.shape, F32),
        scratch_shapes=[pltpu.SemaphoreType.DMA((2,))],
        input_output_aliases={4: 0},
        cost_estimate=cost(0, 8 * (f3.size + brow.size)),
        name="place",
    )(info, spots, f3, brow, out)


def plan(pivots, width, procs, me):
    p0, p1 = pivots[0], pivots[1]
    count = jnp.arange(width, dtype=jnp.int32)
    hit = p0[:, None] == p1[None, :]
    back = p0[:, None] == width + count[None, :]
    src1 = jnp.where(hit.any(0), jnp.sum(jnp.where(hit, count[:, None], 0), 0), p1)
    dest0 = jnp.where(
        back.any(1),
        jnp.sum(jnp.where(back, p1[None, :], 0), 1),
        jnp.where(hit.any(1), -1, p0),
    )
    dest1 = jnp.where(back.any(0), -1, p1)
    src = jnp.concatenate([p0, src1])
    dest = jnp.concatenate([dest0, dest1])
    src_owner = src // width % procs
    src_local = src // width // procs * width + src % width
    dest_owner = jnp.where(dest >= 0, dest // width % procs, -1)
    dest_local = dest // width // procs * width + dest % width
    order = jnp.arange(2 * width, dtype=jnp.int32)
    earlier = order[None, :] < order[:, None]
    same_half = (order[None, :] // width) == (order[:, None] // width)
    src_rank = jnp.sum(
        (earlier & (src_owner[None, :] == src_owner[:, None])).astype(jnp.int32), 1
    )
    dest_rank = jnp.sum(
        (earlier & same_half & (dest_owner[None, :] == dest_owner[:, None])).astype(jnp.int32), 1
    )
    src_most = jnp.max(src_rank) + 1
    dest_most = jnp.max(jnp.where(dest >= 0, dest_rank, -1)) + 1
    return src_owner, src_local, src_rank, dest_owner, dest_local, dest_rank, src_most, dest_most


def factor(cap, fcap, matrix, inv, info, src, dest):
    row_blocks, _, width, blocks, _, _ = matrix.shape
    procs = lax.axis_size("prow")
    chips = lax.axis_size("pcol") // 2
    per = width // LANES
    groups = blocks * per
    rows = row_blocks * width
    me, z = info[0], info[2]
    m2 = matrix.reshape(rows * groups, LANES)
    m4 = matrix.reshape(rows, blocks, per, LANES)
    src_owner, src_local, src_rank = src
    dest_owner, dest_local, dest_rank = dest
    hop = [(q, q + 2) for q in range(2 * chips - 2)]
    swap = [(q, q ^ 1) for q in range(2 * chips)]

    slots = jnp.arange(cap, dtype=jnp.int32)
    mine = (src_owner == me)[None, :] & (src_rank[None, :] == slots[:, None])
    row_list = jnp.sum(jnp.where(mine, src_local[None, :], 0), 1)
    index = src_owner * cap + src_rank

    fslots = jnp.arange(fcap, dtype=jnp.int32)
    owner2 = dest_owner.reshape(2, width)
    rank2 = dest_rank.reshape(2, width)
    local2 = dest_local.reshape(2, width)
    half = jnp.minimum(me, 1)
    to = me ^ jnp.arange(procs, dtype=jnp.int32)
    out_owner = jnp.where(half == 0, owner2[0], owner2[1])
    out_rank = jnp.where(half == 0, rank2[0], rank2[1])
    chosen = (out_owner[None, None, :] == to[:, None, None]) & (
        out_rank[None, None, :] == fslots[None, :, None]
    )
    out_list = jnp.sum(jnp.where(chosen, jnp.arange(width, dtype=jnp.int32), 0), 2)
    landing = (owner2[:, None, :] == me) & (rank2[:, None, :] == fslots[None, :, None])
    spots = (jnp.sum(jnp.where(landing, local2[:, None, :] + 1, 0), 2) - 1).reshape(2 * fcap)

    chunk = rows // CHUNKS
    own, sib = [], []
    for t in range(CHUNKS + chips - 1):
        if t == 0:
            cur = panel(m4, 0, chunk)
        else:
            cur = lax.ppermute(own[-1], "pcol", hop).reshape(chunk, per, LANES)
            if t < CHUNKS:
                cur = pick(info, m4, cur, t * chunk)
        cur = cur.reshape(chunk * per, LANES)
        own.append(cur)
        sib.append(lax.ppermute(cur, "pcol", swap))

    sent = take_rows(row_list, m4).reshape(cap * groups, LANES)
    gathered = lax.all_gather(sent, "prow", axis=0, tiled=True)
    asm, tab = assemble(info, index, gathered.reshape(procs * cap, groups, LANES), width, per)

    outgoing = send_rows(info, out_list, m4)
    bufs = [outgoing[0]]
    for x in range(1, procs):
        pairs = [(s, s ^ x) for s in range(2)]
        moved_buf = lax.ppermute(outgoing[x].reshape(fcap * groups, LANES), "prow", pairs)
        bufs.append(moved_buf.reshape(outgoing[x].shape))
    f4, ftab = fetch(info, bufs)

    def spread(table):
        for h in range(1, chips):
            pairs = [(2 * h - 2, 2 * h), (2 * h - 1, 2 * h + 1)]
            table = jnp.where(z == h, lax.ppermute(table, "pcol", pairs), table)
        return table, lax.ppermute(table, "pcol", swap)

    tab_own, tab_sib = spread(tab.reshape(width * per, LANES))
    uhl, brow, u01 = solve(
        info, asm.reshape(2 * width * groups, LANES), tab_own, tab_sib, inv, groups, per
    )
    ftab_own, ftab_sib = spread(ftab.reshape(2 * fcap * per, LANES))
    fixed = moved(
        info, f4.reshape(2 * fcap * groups, LANES), ftab_own, ftab_sib, inv, u01, uhl, groups, per
    )

    out = None
    for s in range(CHUNKS):
        out = bulk(
            info, own[s : s + chips], sib[s : s + chips], m2, inv, u01, uhl, out, s * chunk, chunk,
            groups, per,
        )
    out = place(
        info,
        spots,
        fixed.reshape(2 * fcap, groups, LANES),
        brow.reshape(2 * width, groups, LANES),
        out.reshape(rows, groups, LANES),
    )
    return out.reshape(matrix.shape)


def shards(matrix, pivots, inverse_blocks):
    width = matrix.shape[2]
    procs = lax.axis_size("prow")
    me = lax.axis_index("prow").astype(jnp.int32)
    mc = lax.axis_index("pcol").astype(jnp.int32)
    info = jnp.stack([me, mc, mc // 2, mc % 2])
    so, sl, sr, do, dl, dr, src_most, dest_most = plan(pivots, width, procs, me)
    mean = 2 * width // procs
    cap = min(2 * width, (mean + 3 * mean // 8 + 7) // 8 * 8)
    fmean = width // procs
    fcap = min(width, (fmean + fmean // 2 + 7) // 8 * 8)
    fits = (src_most <= cap) & (dest_most <= fcap)
    return lax.cond(
        fits,
        functools.partial(factor, cap, fcap),
        functools.partial(factor, 2 * width, width),
        matrix, inverse_blocks, info, (so, sl, sr), (do, dl, dr),
    )


def solution(mesh):
    return jax.shard_map(
        shards,
        mesh=mesh,
        in_specs=(P(None, "prow", None, None, "pcol", None), P(), P()),
        out_specs=P(None, "prow", None, None, "pcol", None),
        check_vma=False,
    )
```

time: 945 us -> 725 us (0.77)
  Pallas kernels: 0 us -> 561 us
  waiting for transfers between devices: 526 us -> 57.2 us
  local copies, waits for them, and re-layouts: 170 us -> 12 us
  other arithmetic: 134 us -> 8.63 us
  matrix products: 93.1 us -> 0 us
  starting transfers between devices: 0.38 us -> 57.6 us
  loops' own time: 0 us -> 9.85 us
    pallas_call x0 -> x23, Pallas kernels: none -> 561 us  [the longest x7 123 us: pick(): pl.pallas_call(functools.partial(pick_kernel, first, recv.shape[0]), in_s...]
    psum x6 -> x0, waiting for transfers between devices: 526 us -> none  [the longest x4 315 us: spread(): return lax.psum(block, axis)]
    unnamed x1 -> x0, other arithmetic: 94.1 us -> none
    dot_general x6 -> x0, matrix products: 93.1 us -> none  [product(): jnp.dot(left, right_side, precision=lax.Precision.HIGHEST, preferred_elem...]
    ppermute x0 -> x32, starting transfers between devices: none -> 57.6 us  [the longest x10 39.8 us: factor(): cur = lax.ppermute(own[-1], 'pcol', hop).reshape(chunk, per, LANES)]
    ppermute x0 -> x32, waiting for transfers between devices: none -> 57.2 us  [the longest x10 57.1 us: factor(): cur = lax.ppermute(own[-1], 'pcol', hop).reshape(chunk, per, LANES)]
    scatter x3 -> x0, local copies, waits for them, and re-layouts: 51 us -> none  [the longest x2 49.5 us: shards(): local_block = local_block.at[target].set(old_rows, mode='drop')]
    reshape x1 -> x0, local copies, waits for them, and re-layouts: 48.3 us -> none  [shards(): return local_block.reshape(full_shape)]
  transfers between devices with their start and end apart: 6 -> 33, of which waited for: 6 -> 6; matrix products, arithmetic and copies ran while one was open for 3% -> 1% of each run, Pallas kernels for 0% -> 57%
where the time goes in v1:
time: 725 us; the launch traced here: 721 us
  Pallas kernels  561 us (77%)
  starting transfers between devices  57.6 us (8%)
  waiting for transfers between devices  57.2 us (8%)
  between operations  15 us (2%)
  local copies, waits for them, and re-layouts  12 us (2%)
  loops' own time  9.85 us (1%)
  other arithmetic  8.63 us (1%)
    pallas_call x7, Pallas kernels, pick(): pl.pallas_call(functools.partial(pick_kernel, first, recv.shape[0]), in_s...  123 us
    pallas_call x1, Pallas kernels, place(): pl.pallas_call(place_kernel, in_specs=[SMEM, SMEM, ANY, ANY, ANY], out_sp...  98.9 us
    pallas_call x8, Pallas kernels, bulk(): pl.pallas_call(functools.partial(bulk_kernel, chips, groups, per, tile, f...  98.2 us
    pallas_call x1, Pallas kernels, send_rows(): pl.pallas_call(send_rows_kernel, in_specs=[SMEM, SMEM, ANY], out_specs=[A...  97.2 us
    ppermute x10, waiting for transfers between devices, factor(): cur = lax.ppermute(own[-1], 'pcol', hop).reshape(chunk, per, LANES)  57.1 us
    pallas_call x1, Pallas kernels, fetch(): pl.pallas_call(fetch_kernel, in_specs=[SMEM] + [ANY] * len(bufs), out_spe...  56.4 us
    pallas_call x1, Pallas kernels, take_rows(): pl.pallas_call(rows_kernel, in_specs=[SMEM, ANY], out_specs=ANY, out_shap...  45.5 us
    ppermute x10, starting transfers between devices, factor(): cur = lax.ppermute(own[-1], 'pcol', hop).reshape(chunk, per, LANES)  39.8 us
  transfers between devices with their start and end apart: 33, of which 6 were waited for; matrix products, arithmetic and copies ran while one was open for 1% of the time, Pallas kernels for 57%

profile of v1, /device:TPU:0, one launch (start us, length us, event | category | flops | bytes accessed | tf_op | source)
XLA Modules:
  0.0 721.1 jit_solution(4648408193333534402)
XLA Ops:
  12.0 702.0 %conditional.1 = (f32[16,1,256,8,1,256]{5,4,3,2,1,0:T(1,128)}) conditional(s32[]{:T(128)} %convert_element_type.11, (s32[]{:T(128)}, s32[512]{0:T(512)S(1)}, s32[512]{0:T(512)S(1)}, s32[512]{0:T(512)S(1)}, f32[16,1,256,8,1,256]{5,4,3,2,1,0:T(1,128)}, /*index=5*/s32[4]{0:T(128)S(1)}, s32[]{:T(128)}, s32[512]{0:T(512)S(1)}, s32[512]{0:T(512)S(1)}, ...), branch_computations={%region_10.14_spmd, %region_14.18_spmd} | conditional | flops 31409979392 | bytes 394236032 | solution.py:571
  21.3 45.5 %take_rows.3 = f32[176,8,2,128]{3,2,1,0:T(2,128)} custom-call(s32[176]{0:T(256)} %select_reduce_fusion.4.list_ref, f32[4096,8,2,128]{3,2,1,0:T(2,128)} %bitcast.98), custom_call_target="tpu_custom_call" | custom-call | bytes 1441792 | tf_op jit(solution)/shard_map/cond/branch_1_fun/take_rows/pallas_call | solution.py:94
  67.0 17.0 %panel.3 = f32[512,2,128]{2,1,0:T(2,128)} custom-call(f32[4096,8,2,128]{3,2,1,0:T(2,128)} %bitcast.99), custom_call_target="tpu_custom_call" | custom-call | bytes 1048576 | tf_op jit(solution)/shard_map/cond/branch_1_fun/panel/pallas_call | solution.py:170
  89.0 11.4 %collective-permute-done.43 = f32[1024,128]{1,0:T(8,128)S(1)} collective-permute-done((f32[1024,128]{1,0:T(8,128)}, f32[1024,128]{1,0:T(8,128)S(1)}, u32[]{:S(2)}, u32[]{:S(2)}) %collective-permute-start.43) | collective-permute-done | bytes 524320 | tf_op jit(solution)/shard_map/cond/branch_1_fun/ppermute | solution.py:509
  101.2 17.5 %pick.21 = f32[512,2,128]{2,1,0:T(2,128)} custom-call(s32[4]{0:T(128)S(1)} %get-tuple-element.74.info_ref, f32[4096,8,2,128]{3,2,1,0:T(2,128)} %bitcast.100, f32[512,2,128]{2,1,0:T(2,128)} %bitcast.221), custom_call_target="tpu_custom_call" | custom-call | bytes 1048576 | tf_op jit(solution)/shard_map/cond/branch_1_fun/pick/pallas_call | solution.py:151
  134.5 17.5 %pick.22 = f32[512,2,128]{2,1,0:T(2,128)} custom-call(s32[4]{0:T(128)S(1)} %get-tuple-element.74.info_ref, f32[4096,8,2,128]{3,2,1,0:T(2,128)} %bitcast.101, f32[512,2,128]{2,1,0:T(2,128)} %bitcast.217), custom_call_target="tpu_custom_call" | custom-call | bytes 1048576 | tf_op jit(solution)/shard_map/cond/branch_1_fun/pick/pallas_call | solution.py:151
  166.9 17.5 %pick.23 = f32[512,2,128]{2,1,0:T(2,128)} custom-call(s32[4]{0:T(128)S(1)} %get-tuple-element.74.info_ref, f32[4096,8,2,128]{3,2,1,0:T(2,128)} %bitcast.102, f32[512,2,128]{2,1,0:T(2,128)} %bitcast.216), custom_call_target="tpu_custom_call" | custom-call | bytes 1048576 | tf_op jit(solution)/shard_map/cond/branch_1_fun/pick/pallas_call | solution.py:151
  189.6 97.2 %send_rows.3 = (f32[96,8,2,128]{3,2,1,0:T(2,128)}, f32[96,8,2,128]{3,2,1,0:T(2,128)}, f32[96,8,2,128]{3,2,1,0:T(2,128)}, f32[96,8,2,128]{3,2,1,0:T(2,128)}) custom-call(s32[4]{0:T(128)S(1)} %get-tuple-element.74.info_ref, s32[4,96]{1,0:T(4,128)} %select_reduce_fusion.3.list_ref, f32[4096,8,2,128]{3,2,1,0:T(2,128)} %bitcast.103), custom_call_target="tpu_custom_call" | custom-call | bytes 6291456 | tf_op jit(solution)/shard_map/cond/branch_1_fun/send_rows/pallas_call | solution.py:125
  293.8 17.5 %pick.24 = f32[512,2,128]{2,1,0:T(2,128)} custom-call(s32[4]{0:T(128)S(1)} %get-tuple-element.74.info_ref, f32[4096,8,2,128]{3,2,1,0:T(2,128)} %bitcast.104, f32[512,2,128]{2,1,0:T(2,128)} %bitcast.215), custom_call_target="tpu_custom_call" | custom-call | bytes 1048576 | tf_op jit(solution)/shard_map/cond/branch_1_fun/pick/pallas_call | solution.py:151
  326.7 56.4 %fetch.3 = (f32[192,8,2,128]{3,2,1,0:T(2,128)}, f32[192,2,128]{2,1,0:T(2,128)}) custom-call(s32[4]{0:T(128)S(1)} %get-tuple-element.74.info_ref, f32[96,8,2,128]{3,2,1,0:T(2,128)} %get-tuple-element.80.rest_0_, f32[96,8,2,128]{3,2,1,0:T(2,128)} %bitcast.205, f32[96,8,2,128]{3,2,1,0:T(2,128)} %bitcast.206, f32[96,8,2,128]{3,2,1,0:T(2,128)} %bitcast.207), custom_call_target="tpu_custom_call" | custom-call | bytes 3145728 | tf_op jit(solution)/shard_map/cond/branch_1_fun/fetch/pallas_call | solution.py:233
  385.2 17.5 %pick.25 = f32[512,2,128]{2,1,0:T(2,128)} custom-call(s32[4]{0:T(128)S(1)} %get-tuple-element.74.info_ref, f32[4096,8,2,128]{3,2,1,0:T(2,128)} %bitcast.105, f32[512,2,128]{2,1,0:T(2,128)} %bitcast.208), custom_call_target="tpu_custom_call" | custom-call | bytes 1048576 | tf_op jit(solution)/shard_map/cond/branch_1_fun/pick/pallas_call | solution.py:151
  405.7 10.7 %collective-permute-done.48 = f32[1024,128]{1,0:T(8,128)S(1)} collective-permute-done((f32[1024,128]{1,0:T(8,128)}, f32[1024,128]{1,0:T(8,128)S(1)}, u32[]{:S(2)}, u32[]{:S(2)}) %collective-permute-start.48) | collective-permute-done | bytes 524320 | tf_op jit(solution)/shard_map/cond/branch_1_fun/ppermute | solution.py:509
  417.1 17.5 %pick.26 = f32[512,2,128]{2,1,0:T(2,128)} custom-call(s32[4]{0:T(128)S(1)} %get-tuple-element.74.info_ref, f32[4096,8,2,128]{3,2,1,0:T(2,128)} %bitcast.106, f32[512,2,128]{2,1,0:T(2,128)} %bitcast.214), custom_call_target="tpu_custom_call" | custom-call | bytes 1048576 | tf_op jit(solution)/shard_map/cond/branch_1_fun/pick/pallas_call | solution.py:151
  451.8 17.5 %pick.27 = f32[512,2,128]{2,1,0:T(2,128)} custom-call(s32[4]{0:T(128)S(1)} %get-tuple-element.74.info_ref, f32[4096,8,2,128]{3,2,1,0:T(2,128)} %bitcast.107, f32[512,2,128]{2,1,0:T(2,128)} %bitcast.211), custom_call_target="tpu_custom_call" | custom-call | bytes 1048576 | tf_op jit(solution)/shard_map/cond/branch_1_fun/pick/pallas_call | solution.py:151
  488.6 11.7 %solve.3 = (bf16[2,512,2048]{2,1,0:T(8,128)(2,1)}, f32[8192,128]{1,0:T(8,128)}, f32[256,256]{1,0:T(8,128)}) custom-call(s32[4]{0:T(128)S(1)} %get-tuple-element.74.info_ref, f32[8192,128]{1,0:T(8,128)} %bitcast.244, f32[512,128]{1,0:T(8,128)} %broadcast_select_fusion.8.own_ref, f32[512,128]{1,0:T(8,128)} %copy-done.79, f32[2,256,256]{2,1,0:T(8,128)S(1)} %copy-done.1), custom_call_target="tpu_custom_call" | custom-call | flops 2415919104 | bytes 12582912 | tf_op jit(solution)/shard_map/cond/branch_1_fun/solve/pallas_call | solution.py:284
  501.0 12.3 %bulk.24.rest_12_ = f32[65536,128]{1,0:T(8,128)} custom-call(s32[4]{0:T(128)S(1)} %get-tuple-element.74.info_ref, f32[1024,128]{1,0:T(8,128)} %bitcast.48.rest_0_, f32[1024,128]{1,0:T(8,128)} %bitcast.50.rest_1_.rest_0_, f32[1024,128]{1,0:T(8,128)} %bitcast.184, f32[1024,128]{1,0:T(8,128)} %bitcast.124, f32[1024,128]{1,0:T(8,128)} %collective-permute-done.63.rest_4_, ...), custom_call_target="tpu_custom_call" | custom-call | flops 3221225472 | bytes 8388608 | tf_op jit(solution)/shard_map/cond/branch_1_fun/bulk/pallas_call | solution.py:342
  517.0 12.3 %bulk.25.rest_12_ = f32[65536,128]{1,0:T(8,128)} custom-call(s32[4]{0:T(128)S(1)} %get-tuple-element.74.info_ref, f32[1024,128]{1,0:T(8,128)} %bitcast.50.rest_1_.rest_0_, f32[1024,128]{1,0:T(8,128)} %bitcast.185, f32[1024,128]{1,0:T(8,128)} %bitcast.125, f32[1024,128]{1,0:T(8,128)} %bitcast.142, ...), custom_call_target="tpu_custom_call", output_to_operand_aliasing={{}: (13, {})} | custom-call | flops 3221225472 | bytes 8388608 | tf_op jit(solution)/shard_map/cond/branch_1_fun/bulk/pallas_call | solution.py:342
  530.2 12.2 %bulk.26.rest_12_ = f32[65536,128]{1,0:T(8,128)} custom-call(s32[4]{0:T(128)S(1)} %get-tuple-element.74.info_ref, f32[1024,128]{1,0:T(8,128)} %bitcast.186, f32[1024,128]{1,0:T(8,128)} %bitcast.126, f32[1024,128]{1,0:T(8,128)} %bitcast.143, f32[1024,128]{1,0:T(8,128)} %bitcast.154, ...), custom_call_target="tpu_custom_call", output_to_operand_aliasing={{}: (13, {})} | custom-call | flops 3221225472 | bytes 8388608 | tf_op jit(solution)/shard_map/cond/branch_1_fun/bulk/pallas_call | solution.py:342
  543.3 12.2 %bulk.27.rest_12_ = f32[65536,128]{1,0:T(8,128)} custom-call(s32[4]{0:T(128)S(1)} %get-tuple-element.74.info_ref, f32[1024,128]{1,0:T(8,128)} %bitcast.127, f32[1024,128]{1,0:T(8,128)} %bitcast.144, f32[1024,128]{1,0:T(8,128)} %bitcast.155, f32[1024,128]{1,0:T(8,128)} %bitcast.166, ...), custom_call_target="tpu_custom_call", output_to_operand_aliasing={{}: (13, {})} | custom-call | flops 3221225472 | bytes 8388608 | tf_op jit(solution)/shard_map/cond/branch_1_fun/bulk/pallas_call | solution.py:342
  556.3 12.4 %bulk.28.rest_12_ = f32[65536,128]{1,0:T(8,128)} custom-call(s32[4]{0:T(128)S(1)} %get-tuple-element.74.info_ref, f32[1024,128]{1,0:T(8,128)} %bitcast.145, f32[1024,128]{1,0:T(8,128)} %bitcast.156, f32[1024,128]{1,0:T(8,128)} %bitcast.167, f32[1024,128]{1,0:T(8,128)} %bitcast.178, f32[1024,128]{1,0:T(8,128)} %copy-done.15, ...), custom_call_target="tpu_custom_call", output_to_operand_aliasing={{}: (13, {})} | custom-call | flops 3221225472 | bytes 8388608 | tf_op jit(solution)/shard_map/cond/branch_1_fun/bulk/pallas_call | solution.py:342
  569.5 12.2 %bulk.29.rest_12_ = f32[65536,128]{1,0:T(8,128)} custom-call(s32[4]{0:T(128)S(1)} %get-tuple-element.74.info_ref, f32[1024,128]{1,0:T(8,128)} %bitcast.157, f32[1024,128]{1,0:T(8,128)} %bitcast.168, f32[1024,128]{1,0:T(8,128)} %bitcast.179, f32[1024,128]{1,0:T(8,128)} %collective-permute-done.50.rest_3_.rest_2_.rest_1_, ...), custom_call_target="tpu_custom_call", output_to_operand_aliasing={{}: (13, {})} | custom-call | flops 3221225472 | bytes 8388608 | tf_op jit(solution)/shard_map/cond/branch_1_fun/bulk/pallas_call | solution.py:342
  582.6 12.2 %bulk.30.rest_12_ = f32[65536,128]{1,0:T(8,128)} custom-call(s32[4]{0:T(128)S(1)} %get-tuple-element.74.info_ref, f32[1024,128]{1,0:T(8,128)} %bitcast.169, f32[1024,128]{1,0:T(8,128)} %bitcast.180, f32[1024,128]{1,0:T(8,128)} %collective-permute-done.50.rest_3_.rest_2_.rest_1_, f32[1024,128]{1,0:T(8,128)} %copy-done.26, ...), custom_call_target="tpu_custom_call", output_to_operand_aliasing={{}: (13, {})} | custom-call | flops 3221225472 | bytes 8388608 | tf_op jit(solution)/shard_map/cond/branch_1_fun/bulk/pallas_call | solution.py:342
  595.7 12.2 %bulk.31 = f32[65536,128]{1,0:T(8,128)} custom-call(s32[4]{0:T(128)S(1)} %get-tuple-element.74.info_ref, f32[1024,128]{1,0:T(8,128)} %bitcast.181, f32[1024,128]{1,0:T(8,128)} %collective-permute-done.50.rest_3_.rest_2_.rest_1_, f32[1024,128]{1,0:T(8,128)} %copy-done.26, f32[1024,128]{1,0:T(8,128)} %copy-done.35, ...), custom_call_target="tpu_custom_call", output_to_operand_aliasing={{}: (13, {})} | custom-call | flops 3221225472 | bytes 8388608 | tf_op jit(solution)/shard_map/cond/branch_1_fun/bulk/pallas_call | solution.py:342
  614.9 98.9 %place.3 = f32[4096,16,128]{2,1,0:T(8,128)} custom-call(s32[4]{0:T(128)S(1)} %get-tuple-element.74.info_ref, s32[192]{0:T(256)} %sub.41.spot_ref, f32[192,16,128]{2,1,0:T(8,128)} %bitcast.193, f32[512,16,128]{2,1,0:T(8,128)} %bitcast.201, f32[4096,16,128]{2,1,0:T(8,128)} %bitcast.118), custom_call_target="tpu_custom_call", output_to_operand_aliasing={{}: (4, {})} | custom-call | bytes 11534336 | tf_op jit(solution)/shard_map/cond/branch_1_fun/place/pallas_call | solution.py:424
  (214 shorter events, 126.5 us)
Async XLA Ops:
  20.6 294.8 %all-gather.5.cloned.1.call-start = ((), (), s32[]{:S(2)}) async-start(), calls=%async_computation.1 | async-start | bytes 7208960 | tf_op jit(solution)/shard_map/cond/branch_1_fun/all_gather | solution.py:517
  184.5 108.4 %collective-permute-start.46 = (f32[1024,128]{1,0:T(8,128)}, f32[1024,128]{1,0:T(8,128)S(1)}, u32[]{:S(2)}, u32[]{:S(2)}) collective-permute-start(f32[1024,128]{1,0:T(8,128)} %bitcast.123), channel_id=1, source_target_pairs={{0,2},{1,3},{2,4},{3,5},{4,6},{5,7},{8,10},{9,11},{10,12},{11,13},... | collective-permute-start | bytes 1572872 | tf_op jit(solution)/shard_map/cond/branch_1_fun/ppermute | solution.py:509
  286.8 38.5 %collective-permute-start.32 = (f32[1536,128]{1,0:T(8,128)}, f32[1536,128]{1,0:T(8,128)S(1)}, u32[]{:S(2)}, u32[]{:S(2)}) collective-permute-start(f32[1536,128]{1,0:T(8,128)} %bitcast.251), channel_id=1, source_target_pairs={{0,8},{8,0},{1,9},{9,1},{2,10},{10,2},{3,11},{11,3},{4,12},{12,4},... | collective-permute-start | bytes 2359304 | tf_op jit(solution)/shard_map/cond/branch_1_fun/ppermute | solution.py:524
  290.2 35.2 %collective-permute-start.33 = (f32[1536,128]{1,0:T(8,128)}, f32[1536,128]{1,0:T(8,128)S(1)}, u32[]{:S(2)}, u32[]{:S(2)}) collective-permute-start(f32[1536,128]{1,0:T(8,128)} %bitcast.250), channel_id=1, source_target_pairs={{0,16},{8,24},{1,17},{9,25},{2,18},{10,26},{3,19},{11,27},{4,20},{... | collective-permute-start | bytes 2359304 | tf_op jit(solution)/shard_map/cond/branch_1_fun/ppermute | solution.py:524
  291.5 33.9 %collective-permute-start.34 = (f32[1536,128]{1,0:T(8,128)}, f32[1536,128]{1,0:T(8,128)S(1)}, u32[]{:S(2)}, u32[]{:S(2)}) collective-permute-start(f32[1536,128]{1,0:T(8,128)} %bitcast.249), channel_id=1, source_target_pairs={{0,24},{8,16},{1,25},{9,17},{2,26},{10,18},{3,27},{11,19},{4,28},{... | collective-permute-start | bytes 2359304 | tf_op jit(solution)/shard_map/cond/branch_1_fun/ppermute | solution.py:524
  311.3 73.1 %collective-permute-start.47 = (f32[1024,128]{1,0:T(8,128)}, f32[1024,128]{1,0:T(8,128)S(1)}, u32[]{:S(2)}, u32[]{:S(2)}) collective-permute-start(f32[1024,128]{1,0:T(8,128)} %bitcast.141), channel_id=1, source_target_pairs={{0,2},{1,3},{2,4},{3,5},{4,6},{5,7},{8,10},{9,11},{10,12},{11,13},... | collective-permute-start | bytes 1572872 | tf_op jit(solution)/shard_map/cond/branch_1_fun/ppermute | solution.py:509
  321.7 82.4 %collective-permute-start.39 = (f32[512,128]{1,0:T(8,128)}, f32[512,128]{1,0:T(8,128)S(1)}, u32[]{:S(2)}, u32[]{:S(2)}) collective-permute-start(f32[512,128]{1,0:T(8,128)} %bitcast.224), channel_id=1, source_target_pairs={{0,2},{1,3},{8,10},{9,11},{16,18},{17,19},{24,26},{25,27}} | collective-permute-start | bytes 786440 | tf_op jit(solution)/shard_map/cond/branch_1_fun/ppermute | solution.py:531
  325.3 149.9 %collective-permute-start.63 = (f32[1024,128]{1,0:T(8,128)}, f32[1024,128]{1,0:T(8,128)}, u32[]{:S(2)}, u32[]{:S(2)}) collective-permute-start(f32[1024,128]{1,0:T(8,128)} %bitcast.48.rest_0_), channel_id=1, source_target_pairs={{0,1},{1,0},{2,3},{3,2},{4,5},{5,4},{6,7},{7,6},{8,9},{9,8},{10,11... | collective-permute-start | bytes 1572872 | tf_op jit(solution)/shard_map/cond/branch_1_fun/ppermute | solution.py:514
  404.2 34.9 %collective-permute-start.40 = (f32[512,128]{1,0:T(8,128)S(1)}, f32[512,128]{1,0:T(8,128)S(1)}, u32[]{:S(2)}, u32[]{:S(2)}) collective-permute-start(f32[512,128]{1,0:T(8,128)S(1)} %broadcast_select_fusion.6), channel_id=1, source_target_pairs={{2,4},{3,5},{10,12},{11,13},{18,20},{19,21},{26,28},{27,29}} | collective-permute-start | bytes 786440 | tf_op jit(solution)/shard_map/cond/branch_1_fun/ppermute | solution.py:531
  405.0 35.7 %collective-permute-start.36 = (f32[384,128]{1,0:T(8,128)S(1)}, f32[384,128]{1,0:T(8,128)S(1)}, u32[]{:S(2)}, u32[]{:S(2)}) collective-permute-start(f32[384,128]{1,0:T(8,128)S(1)} %broadcast_select_fusion.9), channel_id=1, source_target_pairs={{2,4},{3,5},{10,12},{11,13},{18,20},{19,21},{26,28},{27,29}} | collective-permute-start | bytes 589832 | tf_op jit(solution)/shard_map/cond/branch_1_fun/ppermute | solution.py:531
  439.1 30.3 %collective-permute-start.41 = (f32[512,128]{1,0:T(8,128)S(1)}, f32[512,128]{1,0:T(8,128)}, u32[]{:S(2)}, u32[]{:S(2)}) collective-permute-start(f32[512,128]{1,0:T(8,128)S(1)} %broadcast_select_fusion.7), channel_id=1, source_target_pairs={{4,6},{5,7},{12,14},{13,15},{20,22},{21,23},{28,30},{29,31}} | collective-permute-start | bytes 786440 | tf_op jit(solution)/shard_map/cond/branch_1_fun/ppermute | solution.py:531
  440.6 59.7 %collective-permute-start.62 = (f32[1024,128]{1,0:T(8,128)}, f32[1024,128]{1,0:T(8,128)}, u32[]{:S(2)}, u32[]{:S(2)}) collective-permute-start(f32[1024,128]{1,0:T(8,128)} %bitcast.50.rest_1_.rest_0_), channel_id=1, source_target_pairs={{0,1},{1,0},{2,3},{3,2},{4,5},{5,4},{6,7},{7,6},{8,9},{9,8},{10,11... | collective-permute-start | bytes 1572872 | tf_op jit(solution)/shard_map/cond/branch_1_fun/ppermute | solution.py:514
  440.7 59.8 %collective-permute-start.61 = (f32[1024,128]{1,0:T(8,128)S(1)}, f32[1024,128]{1,0:T(8,128)}, u32[]{:S(2)}, u32[]{:S(2)}) collective-permute-start(f32[1024,128]{1,0:T(8,128)S(1)} %bitcast.187), channel_id=1, source_target_pairs={{0,1},{1,0},{2,3},{3,2},{4,5},{5,4},{6,7},{7,6},{8,9},{9,8},{10,11... | collective-permute-start | bytes 1572872 | tf_op jit(solution)/shard_map/cond/branch_1_fun/ppermute | solution.py:514
  475.2 25.7 %collective-permute-start.60 = (f32[1024,128]{1,0:T(8,128)S(1)}, f32[1024,128]{1,0:T(8,128)}, u32[]{:S(2)}, u32[]{:S(2)}) collective-permute-start(f32[1024,128]{1,0:T(8,128)S(1)} %bitcast.128), channel_id=1, source_target_pairs={{0,1},{1,0},{2,3},{3,2},{4,5},{5,4},{6,7},{7,6},{8,9},{9,8},{10,11... | collective-permute-start | bytes 1572872 | tf_op jit(solution)/shard_map/cond/branch_1_fun/ppermute | solution.py:514
  484.2 29.2 %collective-permute-start.59 = (f32[1024,128]{1,0:T(8,128)S(1)}, f32[1024,128]{1,0:T(8,128)S(1)}, u32[]{:S(2)}, u32[]{:S(2)}) collective-permute-start(f32[1024,128]{1,0:T(8,128)S(1)} %bitcast.146), channel_id=1, source_target_pairs={{0,1},{1,0},{2,3},{3,2},{4,5},{5,4},{6,7},{7,6},{8,9},{9,8},{10,11... | collective-permute-start | bytes 1572872 | tf_op jit(solution)/shard_map/cond/branch_1_fun/ppermute | solution.py:514
  484.2 29.5 %collective-permute-start.51 = (f32[1024,128]{1,0:T(8,128)}, f32[1024,128]{1,0:T(8,128)S(1)}, u32[]{:S(2)}, u32[]{:S(2)}) collective-permute-start(f32[1024,128]{1,0:T(8,128)} %collective-permute-done.50.rest_3_.rest_2_.rest_1_), channel_id=1, source_target_pairs={{0,2},{1,3},{2,4},{3,5},{4,6},{5,7},{8,10},{9,11},{10,12},{11,13},... | collective-permute-start | bytes 1572872 | tf_op jit(solution)/shard_map/cond/branch_1_fun/ppermute | solution.py:509
  500.3 107.7 %collective-permute-start.38 = (f32[384,128]{1,0:T(8,128)}, f32[384,128]{1,0:T(8,128)}, u32[]{:S(2)}, u32[]{:S(2)}) collective-permute-start(f32[384,128]{1,0:T(8,128)} %broadcast_select_fusion.11.own_ref), channel_id=1, source_target_pairs={{0,1},{1,0},{2,3},{3,2},{4,5},{5,4},{6,7},{7,6},{8,9},{9,8},{10,11... | collective-permute-start | bytes 589832 | tf_op jit(solution)/shard_map/cond/branch_1_fun/ppermute | solution.py:532
  500.5 28.8 %collective-permute-start.58 = (f32[1024,128]{1,0:T(8,128)S(1)}, f32[1024,128]{1,0:T(8,128)S(1)}, u32[]{:S(2)}, u32[]{:S(2)}) collective-permute-start(f32[1024,128]{1,0:T(8,128)S(1)} %bitcast.158), channel_id=1, source_target_pairs={{0,1},{1,0},{2,3},{3,2},{4,5},{5,4},{6,7},{7,6},{8,9},{9,8},{10,11... | collective-permute-start | bytes 1572872 | tf_op jit(solution)/shard_map/cond/branch_1_fun/ppermute | solution.py:514
  500.8 41.6 %collective-permute-start.57 = (f32[1024,128]{1,0:T(8,128)S(1)}, f32[1024,128]{1,0:T(8,128)S(1)}, u32[]{:S(2)}, u32[]{:S(2)}) collective-permute-start(f32[1024,128]{1,0:T(8,128)S(1)} %bitcast.170), channel_id=1, source_target_pairs={{0,1},{1,0},{2,3},{3,2},{4,5},{5,4},{6,7},{7,6},{8,9},{9,8},{10,11... | collective-permute-start | bytes 1572872 | tf_op jit(solution)/shard_map/cond/branch_1_fun/ppermute | solution.py:514
  513.3 42.2 %collective-permute-start.53 = (f32[1024,128]{1,0:T(8,128)S(1)}, f32[1024,128]{1,0:T(8,128)S(1)}, u32[]{:S(2)}, u32[]{:S(2)}) collective-permute-start(f32[1024,128]{1,0:T(8,128)S(1)} %bitcast.182), channel_id=1, source_target_pairs={{0,1},{1,0},{2,3},{3,2},{4,5},{5,4},{6,7},{7,6},{8,9},{9,8},{10,11... | collective-permute-start | bytes 1572872 | tf_op jit(solution)/shard_map/cond/branch_1_fun/ppermute | solution.py:514
  513.7 28.8 %collective-permute-start.52 = (f32[1024,128]{1,0:T(8,128)S(1)}, f32[1024,128]{1,0:T(8,128)S(1)}, u32[]{:S(2)}, u32[]{:S(2)}) collective-permute-start(f32[1024,128]{1,0:T(8,128)S(1)} %collective-permute-done.51.rest_3_.rest_2_), channel_id=1, source_target_pairs={{0,2},{1,3},{2,4},{3,5},{4,6},{5,7},{8,10},{9,11},{10,12},{11,13},... | collective-permute-start | bytes 1572872 | tf_op jit(solution)/shard_map/cond/branch_1_fun/ppermute | solution.py:509
  529.3 39.4 %collective-permute-start.54 = (f32[1024,128]{1,0:T(8,128)}, f32[1024,128]{1,0:T(8,128)S(1)}, u32[]{:S(2)}, u32[]{:S(2)}) collective-permute-start(f32[1024,128]{1,0:T(8,128)} %collective-permute-done.50.rest_3_.rest_2_.rest_1_), channel_id=1, source_target_pairs={{0,1},{1,0},{2,3},{3,2},{4,5},{5,4},{6,7},{7,6},{8,9},{9,8},{10,11... | collective-permute-start | bytes 1572872 | tf_op jit(solution)/shard_map/cond/branch_1_fun/ppermute | solution.py:514
  542.4 39.4 %collective-permute-start.55 = (f32[1024,128]{1,0:T(8,128)S(1)}, f32[1024,128]{1,0:T(8,128)S(1)}, u32[]{:S(2)}, u32[]{:S(2)}) collective-permute-start(f32[1024,128]{1,0:T(8,128)S(1)} %collective-permute-done.51.rest_3_.rest_2_), channel_id=1, source_target_pairs={{0,1},{1,0},{2,3},{3,2},{4,5},{5,4},{6,7},{7,6},{8,9},{9,8},{10,11... | collective-permute-start | bytes 1572872 | tf_op jit(solution)/shard_map/cond/branch_1_fun/ppermute | solution.py:514
  542.5 52.4 %collective-permute-start.56 = (f32[1024,128]{1,0:T(8,128)S(1)}, f32[1024,128]{1,0:T(8,128)S(1)}, u32[]{:S(2)}, u32[]{:S(2)}) collective-permute-start(f32[1024,128]{1,0:T(8,128)S(1)} %collective-permute-done.52.rest_3_), channel_id=1, source_target_pairs={{0,1},{1,0},{2,3},{3,2},{4,5},{5,4},{6,7},{7,6},{8,9},{9,8},{10,11... | collective-permute-start | bytes 1572872 | tf_op jit(solution)/shard_map/cond/branch_1_fun/ppermute | solution.py:514
  (60 other events, 1486.0 us)
Sparse Core Ops, SparseCore 0:
  67.1 68.4 all-gather.4

commit v2 on v1

v2 whole, which is shorter than its diff:
```python
import functools

import jax
import jax.numpy as jnp
from jax import lax
from jax.experimental import pallas as pl
from jax.experimental.pallas import tpu as pltpu
from jax.sharding import PartitionSpec as P

LANES = 128
CHUNKS = 16
CHAINS = 2
TILE = 256
F32 = jnp.float32
BF16 = jnp.bfloat16
ANY = pl.BlockSpec(memory_space=pl.ANY)
VMEM = pl.BlockSpec(memory_space=pltpu.VMEM)
SMEM = pl.BlockSpec(memory_space=pltpu.SMEM)
PARAMS = pltpu.CompilerParams(vmem_limit_bytes=56 << 20)


def cost(flops, nbytes):
    return pl.CostEstimate(flops=int(flops), bytes_accessed=int(nbytes), transcendentals=0)


def split(x):
    high = x.astype(BF16)
    return high, (x - high.astype(F32)).astype(BF16)


def dot3(left, right):
    out = jnp.dot(left[0], right[0], preferred_element_type=F32)
    out += jnp.dot(left[0], right[1], preferred_element_type=F32)
    return out + jnp.dot(left[1], right[0], preferred_element_type=F32)


def upper(packed):
    row = lax.broadcasted_iota(jnp.int32, packed.shape, 0)
    col = lax.broadcasted_iota(jnp.int32, packed.shape, 1)
    return jnp.where(col >= row, packed, 0.0)


def unit_lower(packed):
    row = lax.broadcasted_iota(jnp.int32, packed.shape, 0)
    col = lax.broadcasted_iota(jnp.int32, packed.shape, 1)
    return jnp.where(col < row, packed, jnp.where(col == row, 1.0, 0.0))


def get_block(ref, start, count, pitch, block, per):
    parts = [ref[pl.ds(start * pitch + block * per + h, count, stride=pitch), :] for h in range(per)]
    return jnp.concatenate(parts, axis=1)


def put_block(ref, start, count, pitch, block, per, value):
    for h in range(per):
        ref[pl.ds(start * pitch + block * per + h, count, stride=pitch), :] = value[
            :, h * LANES : (h + 1) * LANES
        ]


def update_rows(count, groups, per, mc, c0, c1, inv_ref, u01_ref, uhl_ref, s_ref, get, put):
    width = per * LANES
    pitch = groups + 1
    l0 = dot3(split(c0), split(upper(inv_ref[0])))
    l0s = split(l0)
    rest = c1 - dot3(l0s, split(u01_ref[...]))
    l1 = dot3(split(rest), split(upper(inv_ref[1])))
    l1s = split(l1)
    high = jnp.concatenate([l0s[0], l1s[0]], axis=1)
    low = jnp.concatenate([l0s[1], l1s[1]], axis=1)
    for block in range(groups // per):
        cols = slice(block * width, (block + 1) * width)
        acc = dot3((high, low), (uhl_ref[0, :, cols], uhl_ref[1, :, cols]))
        if block == 0:
            acc = jnp.where(mc == 0, -l0, jnp.where(mc == 1, -l1, acc))
        put_block(s_ref, 0, count, pitch, block, per, acc)
    drop = (lax.broadcasted_iota(jnp.int32, (groups, LANES), 0) < per) & (mc < 2)

    def step(i, carry):
        put(i, jnp.where(drop, 0.0, get(i)) - s_ref[pl.ds(i * pitch, groups), :])
        return carry

    lax.fori_loop(0, count, step, 0, unroll=8)


def panel(m4, first, count, rows):
    shape = (rows,) + m4.shape[2:]

    def kernel(m_ref, *rest):
        outs, sem = rest[:count], rest[count]
        copies = [
            pltpu.make_async_copy(m_ref.at[pl.ds((first + k) * rows, rows), 0], outs[k], sem.at[k])
            for k in range(count)
        ]
        for copy in copies:
            copy.start()
        for copy in copies:
            copy.wait()

    return pl.pallas_call(
        kernel,
        in_specs=[ANY],
        out_specs=[VMEM] * count,
        out_shape=[jax.ShapeDtypeStruct(shape, F32)] * count,
        scratch_shapes=[pltpu.SemaphoreType.DMA((count,))],
        compiler_params=PARAMS,
        cost_estimate=cost(0, 8 * count * rows * shape[1] * shape[2]),
        name="panel",
    )(m4)


def collect_kernel(procs, per, info_ref, list_ref, out_list_ref, m_ref, *rest):
    a_ref, b_ref = rest[:2]
    out_refs, head_refs = rest[2 : 2 + procs], rest[2 + procs : 2 + 2 * procs]
    row_ref, top_ref, sem = rest[2 + 2 * procs :]
    cap, groups, _ = row_ref.shape
    width = top_ref.shape[0]
    fcap = out_refs[0].shape[0]
    top = pltpu.make_async_copy(m_ref.at[pl.ds(0, width)], top_ref, sem.at[0])
    top.start()

    def fetch(k, carry):
        pltpu.make_async_copy(m_ref.at[list_ref[k]], row_ref.at[k], sem.at[1]).start()
        return carry

    lax.fori_loop(0, cap, fetch, 0)
    top.wait()

    @pl.when(info_ref[0] < 2)
    def _():
        for x in range(procs):

            def give(k, carry):
                row = top_ref[out_list_ref[x, k]]
                out_refs[x][k] = row
                head_refs[x][cap + k] = row[0:per]
                return carry

            lax.fori_loop(0, fcap, give, 0, unroll=4)

    pltpu.make_async_copy(row_ref, row_ref, sem.at[1]).wait()

    def keep(k, carry):
        row = row_ref[k]
        a_ref[k] = row[: groups // 2]
        b_ref[k] = row[groups // 2 :]
        for x in range(procs):
            head_refs[x][k] = row[0:per]
        return carry

    lax.fori_loop(0, cap, keep, 0, unroll=2)


def collect(info, row_list, out_list, m3, per, width):
    cap = row_list.shape[0]
    procs, fcap = out_list.shape
    groups = m3.shape[1]
    half = jax.ShapeDtypeStruct((cap, groups // 2, LANES), F32)
    out = jax.ShapeDtypeStruct((fcap, groups, LANES), F32)
    head = jax.ShapeDtypeStruct((cap + fcap, per, LANES), F32)
    outs = pl.pallas_call(
        functools.partial(collect_kernel, procs, per),
        in_specs=[SMEM, SMEM, SMEM, ANY],
        out_specs=[VMEM] * (2 + 2 * procs),
        out_shape=[half, half] + [out] * procs + [head] * procs,
        scratch_shapes=[
            pltpu.VMEM((cap, groups, LANES), F32),
            pltpu.VMEM((width, groups, LANES), F32),
            pltpu.SemaphoreType.DMA((2,)),
        ],
        compiler_params=PARAMS,
        cost_estimate=cost(0, 16 * (cap + procs * fcap) * groups * LANES),
        name="collect",
    )(info, row_list, out_list, m3)
    return outs[:2], outs[2 : 2 + procs], outs[2 + procs :]


def tables_kernel(procs, cap, info_ref, owner_ref, rank_ref, *rest):
    ins = rest[:procs]
    g_ref, f_ref, buf_ref, sem = rest[procs:]
    width = g_ref.shape[0]
    fcap = f_ref.shape[0] // 2
    copies = [
        pltpu.make_async_copy(ins[x], buf_ref.at[info_ref[0] ^ x], sem.at[x]) for x in range(procs)
    ]
    for copy in copies:
        copy.start()
    for copy in copies:
        copy.wait()
    base = jnp.where(info_ref[3] == 0, width, 0)

    def pivot(k, carry):
        g_ref[k] = buf_ref[owner_ref[base + k], rank_ref[base + k]]
        return carry

    lax.fori_loop(0, width, pivot, 0, unroll=4)
    for source in range(2):

        def other(k, carry):
            f_ref[source * fcap + k] = buf_ref[source, cap + k]
            return carry

        lax.fori_loop(0, fcap, other, 0, unroll=4)


def tables(info, owner, rank, heads, cap, width):
    procs = len(heads)
    both, per, _ = heads[0].shape
    fcap = both - cap
    return pl.pallas_call(
        functools.partial(tables_kernel, procs, cap),
        in_specs=[SMEM, SMEM, SMEM] + [ANY] * procs,
        out_specs=[VMEM, VMEM],
        out_shape=[
            jax.ShapeDtypeStruct((width, per, LANES), F32),
            jax.ShapeDtypeStruct((2 * fcap, per, LANES), F32),
        ],
        scratch_shapes=[
            pltpu.VMEM((procs, both, per, LANES), F32),
            pltpu.SemaphoreType.DMA((procs,)),
        ],
        compiler_params=PARAMS,
        cost_estimate=cost(0, 8 * procs * heads[0].size),
        name="tables",
    )(info, owner, rank, *heads)


def solve_kernel(procs, order_a, order_b, groups, per, info_ref, owner_ref, rank_ref, *rest):
    a_ins, b_ins = rest[:procs], rest[procs : 2 * procs]
    own_ref, sib_ref, inv_ref, uhl_ref, brow_ref, u01_ref, a_ref, b_ref, s_ref, sem = rest[
        2 * procs :
    ]
    width = per * LANES
    pitch = groups + 1
    me, mc = info_ref[0], info_ref[1]
    even = info_ref[3] == 0
    copies = []
    for n in range(procs):
        copies.append(pltpu.make_async_copy(a_ins[n], a_ref.at[me ^ order_a[n]], sem.at[n]))
        copies.append(pltpu.make_async_copy(b_ins[n], b_ref.at[me ^ order_b[n]], sem.at[procs + n]))
    for copy in copies:
        copy.start()
    own = get_block(own_ref, 0, width, per, 0, per)
    sib = get_block(sib_ref, 0, width, per, 0, per)
    z1c0 = jnp.where(even, own, sib)
    g0c1 = jnp.where(even, sib, own)
    low0 = split(unit_lower(inv_ref[0]))
    low1 = split(unit_lower(inv_ref[1]))
    l01 = dot3(split(z1c0), split(upper(inv_ref[0])))
    l01s = split(l01)
    u01_ref[...] = dot3(low0, split(g0c1))
    for copy in copies:
        copy.wait()

    def line_up(k, carry):
        owner, rank = owner_ref[k], rank_ref[k]
        s_ref[pl.ds(k * pitch, groups // 2), :] = a_ref[owner, rank]
        s_ref[pl.ds(k * pitch + groups // 2, groups // 2), :] = b_ref[owner, rank]
        return carry

    lax.fori_loop(0, 2 * width, line_up, 0, unroll=4)
    for block in range(groups // per):
        cols = slice(block * width, (block + 1) * width)
        g0 = get_block(s_ref, 0, width, pitch, block, per)
        z1 = get_block(s_ref, width, width, pitch, block, per)
        u0 = dot3(low0, split(g0))
        u0s = split(u0)
        a1 = z1 - dot3(l01s, u0s)
        u1 = dot3(low1, split(a1))
        u1s = split(u1)
        for part in range(2):
            uhl_ref[part, :width, cols] = u0s[part]
            uhl_ref[part, width:, cols] = u1s[part]
        if block == 0:
            top = jnp.where(mc == 0, g0, u0)
            mid = jnp.where(mc == 0, l01, jnp.where(mc == 1, a1, u1))
        else:
            top, mid = u0, u1
        put_block(s_ref, 0, width, pitch, block, per, top)
        put_block(s_ref, width, width, pitch, block, per, mid)

    def lay_out(k, carry):
        brow_ref[k] = s_ref[pl.ds(k * pitch, groups), :]
        return carry

    lax.fori_loop(0, 2 * width, lay_out, 0, unroll=4)


def solve(info, owner, rank, a_bufs, b_bufs, order_a, order_b, own, sib, inv, groups, per):
    procs = len(a_bufs)
    width = per * LANES
    cols = groups * LANES
    half = pltpu.VMEM((procs,) + a_bufs[0].shape, F32)
    return pl.pallas_call(
        functools.partial(solve_kernel, procs, order_a, order_b, groups, per),
        in_specs=[SMEM, SMEM, SMEM] + [ANY] * (2 * procs) + [VMEM] * 3,
        out_specs=[VMEM, VMEM, VMEM],
        out_shape=[
            jax.ShapeDtypeStruct((2, 2 * width, cols), BF16),
            jax.ShapeDtypeStruct((2 * width, groups, LANES), F32),
            jax.ShapeDtypeStruct((width, width), F32),
        ],
        scratch_shapes=[
            half,
            half,
            pltpu.VMEM((2 * width * (groups + 1), LANES), F32),
            pltpu.SemaphoreType.DMA((2 * procs,)),
        ],
        compiler_params=PARAMS,
        cost_estimate=cost(18 * width * width * cols, 24 * width * cols),
        name="solve",
    )(info, owner, rank, *a_bufs, *b_bufs, own, sib, inv)


def make_bulk_kernel(chips, count, chunk, tile, groups, per):
    def kernel(info_ref, *rest):
        bufs = rest[: 2 * chips * count]
        m_ref, inv_ref, u01_ref, uhl_ref = rest[2 * chips * count : 2 * chips * count + 4]
        o_ref, c0_ref, c1_ref, s_ref, sem = rest[-5:]
        step = pl.program_id(0)

        @pl.when(step == 0)
        def _():
            for h in range(chips):
                for core in range(2):

                    @pl.when((info_ref[2] == h) & (info_ref[3] == core))
                    def _():
                        copies = []
                        for n in range(count):
                            own, sib = bufs[2 * n * chips + h], bufs[(2 * n + 1) * chips + h]
                            first, second = (own, sib) if core == 0 else (sib, own)
                            spot = pl.ds(n * chunk * per, chunk * per)
                            copies.append(
                                pltpu.make_async_copy(first, c0_ref.at[spot], sem.at[2 * n])
                            )
                            copies.append(
                                pltpu.make_async_copy(second, c1_ref.at[spot], sem.at[2 * n + 1])
                            )
                        for copy in copies:
                            copy.start()
                        for copy in copies:
                            copy.wait()

        def get(i):
            return m_ref[pl.ds(pl.multiple_of(i * groups, groups), groups), :]

        def put(i, value):
            o_ref[pl.ds(pl.multiple_of(i * groups, groups), groups), :] = value

        c0 = get_block(c0_ref, step * tile, tile, per, 0, per)
        c1 = get_block(c1_ref, step * tile, tile, per, 0, per)
        update_rows(
            tile, groups, per, info_ref[1], c0, c1, inv_ref, u01_ref, uhl_ref, s_ref, get, put
        )

    return kernel


def bulk(info, bufs, m2, inv, u01, uhl, out, first, count, chunk, groups, per):
    chips = len(bufs) // (2 * count)
    tile = min(TILE, chunk)
    rows = count * chunk
    base = first // tile
    width = per * LANES
    cols = groups * LANES
    block = pl.BlockSpec((tile * groups, LANES), lambda i: (base + i, 0))
    in_specs = [SMEM] + [ANY] * len(bufs) + [block, VMEM, VMEM, VMEM]
    args = [info, *bufs, m2, inv, u01, uhl]
    aliases = {}
    if out is not None:
        in_specs.append(ANY)
        aliases = {len(args): 0}
        args.append(out)
    return pl.pallas_call(
        make_bulk_kernel(chips, count, chunk, tile, groups, per),
        grid=(rows // tile,),
        in_specs=in_specs,
        out_specs=block,
        out_shape=jax.ShapeDtypeStruct(m2.shape, F32),
        scratch_shapes=[
            pltpu.VMEM((rows * per, LANES), F32),
            pltpu.VMEM((rows * per, LANES), F32),
            pltpu.VMEM((tile * (groups + 1), LANES), F32),
            pltpu.SemaphoreType.DMA((2 * count,)),
        ],
        input_output_aliases=aliases,
        compiler_params=PARAMS,
        cost_estimate=cost(12 * rows * width * cols, 8 * rows * cols),
        name="bulk",
    )(*args)


def moved_kernel(procs, groups, per, info_ref, *rest):
    ins = rest[:procs]
    own_ref, sib_ref, inv_ref, u01_ref, uhl_ref, o_ref, f_ref, s_ref, sem = rest[procs:]
    rows = f_ref.shape[0]
    for source in range(2):
        spot = pl.ds(source * (rows // 2), rows // 2)
        for x in range(procs):

            @pl.when((info_ref[0] ^ source) == x)
            def _():
                copy = pltpu.make_async_copy(ins[x], f_ref.at[spot], sem)
                copy.start()
                copy.wait()

    def get(i):
        return f_ref[i]

    def put(i, value):
        o_ref[i] = value

    even = info_ref[3] == 0
    own = get_block(own_ref, 0, rows, per, 0, per)
    sib = get_block(sib_ref, 0, rows, per, 0, per)
    c0 = jnp.where(even, own, sib)
    c1 = jnp.where(even, sib, own)
    update_rows(rows, groups, per, info_ref[1], c0, c1, inv_ref, u01_ref, uhl_ref, s_ref, get, put)


def moved(info, bufs, own, sib, inv, u01, uhl, per):
    fcap, groups, _ = bufs[0].shape
    rows = 2 * fcap
    return pl.pallas_call(
        functools.partial(moved_kernel, len(bufs), groups, per),
        in_specs=[SMEM] + [ANY] * len(bufs) + [VMEM] * 5,
        out_specs=VMEM,
        out_shape=jax.ShapeDtypeStruct((rows, groups, LANES), F32),
        scratch_shapes=[
            pltpu.VMEM((rows, groups, LANES), F32),
            pltpu.VMEM((rows * (groups + 1), LANES), F32),
            pltpu.SemaphoreType.DMA,
        ],
        compiler_params=PARAMS,
        cost_estimate=cost(12 * rows * per * groups * LANES * LANES, 8 * rows * groups * LANES),
        name="moved",
    )(info, *bufs, own, sib, inv, u01, uhl)


def place_kernel(info_ref, spot_ref, f_ref, brow_ref, _, o_ref, sem):
    width = brow_ref.shape[0] // 2
    count = f_ref.shape[0]

    def put(k):
        return pltpu.make_async_copy(f_ref.at[k], o_ref.at[spot_ref[k]], sem.at[0])

    def start(k, carry):
        @pl.when(spot_ref[k] >= 0)
        def _():
            put(k).start()

        return carry

    def finish(k, carry):
        @pl.when(spot_ref[k] >= 0)
        def _():
            put(k).wait()

        return carry

    source = jnp.minimum(info_ref[0], 1)
    top = pltpu.make_async_copy(
        brow_ref.at[pl.ds(source * width, width)], o_ref.at[pl.ds(0, width)], sem.at[1]
    )

    @pl.when(info_ref[0] < 2)
    def _():
        top.start()

    lax.fori_loop(0, count, start, 0)
    lax.fori_loop(0, count, finish, 0)

    @pl.when(info_ref[0] < 2)
    def _():
        top.wait()


def place(info, spots, f3, brow, out):
    return pl.pallas_call(
        place_kernel,
        in_specs=[SMEM, SMEM, VMEM, VMEM, ANY],
        out_specs=ANY,
        out_shape=jax.ShapeDtypeStruct(out.shape, F32),
        scratch_shapes=[pltpu.SemaphoreType.DMA((2,))],
        input_output_aliases={4: 0},
        compiler_params=PARAMS,
        cost_estimate=cost(0, 8 * (f3.size + brow.size)),
        name="place",
    )(info, spots, f3, brow, out)


def plan(pivots, width, procs, me):
    p0, p1 = pivots[0], pivots[1]
    count = jnp.arange(width, dtype=jnp.int32)
    hit = p0[:, None] == p1[None, :]
    back = p0[:, None] == width + count[None, :]
    src1 = jnp.where(hit.any(0), jnp.sum(jnp.where(hit, count[:, None], 0), 0), p1)
    dest0 = jnp.where(
        back.any(1),
        jnp.sum(jnp.where(back, p1[None, :], 0), 1),
        jnp.where(hit.any(1), -1, p0),
    )
    dest1 = jnp.where(back.any(0), -1, p1)
    src = jnp.concatenate([p0, src1])
    dest = jnp.concatenate([dest0, dest1])
    src_owner = src // width % procs
    src_local = src // width // procs * width + src % width
    dest_owner = jnp.where(dest >= 0, dest // width % procs, -1)
    dest_local = dest // width // procs * width + dest % width
    order = jnp.arange(2 * width, dtype=jnp.int32)
    earlier = order[None, :] < order[:, None]
    same_half = (order[None, :] // width) == (order[:, None] // width)
    src_rank = jnp.sum(
        (earlier & (src_owner[None, :] == src_owner[:, None])).astype(jnp.int32), 1
    )
    dest_rank = jnp.sum(
        (earlier & same_half & (dest_owner[None, :] == dest_owner[:, None])).astype(jnp.int32), 1
    )
    src_most = jnp.max(src_rank) + 1
    dest_most = jnp.max(jnp.where(dest >= 0, dest_rank, -1)) + 1
    return src_owner, src_local, src_rank, dest_owner, dest_local, dest_rank, src_most, dest_most


def flip(procs, x):
    return [(s, s ^ x) for s in range(procs)]


def send(value, axis, pairs):
    flat = value.reshape(-1, LANES)
    return lax.ppermute(flat, axis, pairs).reshape(value.shape)


def exchange(cap, fcap, m3, width, info, src, dest):
    per = width // LANES
    procs = lax.axis_size("prow")
    me = info[0]
    src_owner, src_local, src_rank = src
    dest_owner, dest_local, dest_rank = dest

    src_rank = jnp.minimum(src_rank, cap - 1)
    slots = jnp.arange(cap, dtype=jnp.int32)
    mine = (src_owner == me)[None, :] & (src_rank[None, :] == slots[:, None])
    row_list = jnp.max(jnp.where(mine, src_local[None, :], 0), 1)

    fslots = jnp.arange(fcap, dtype=jnp.int32)
    owner2 = dest_owner.reshape(2, width)
    rank2 = dest_rank.reshape(2, width)
    local2 = dest_local.reshape(2, width)
    to = me ^ jnp.arange(procs, dtype=jnp.int32)
    out_owner = jnp.where(me == 0, owner2[0], owner2[1])
    out_rank = jnp.where(me == 0, rank2[0], rank2[1])
    chosen = (out_owner[None, None, :] == to[:, None, None]) & (
        out_rank[None, None, :] == fslots[None, :, None]
    )
    out_list = jnp.sum(jnp.where(chosen, jnp.arange(width, dtype=jnp.int32), 0), 2)
    landing = (owner2[:, None, :] == me) & (rank2[:, None, :] == fslots[None, :, None])
    spots = (jnp.sum(jnp.where(landing, local2[:, None, :] + 1, 0), 2) - 1).reshape(2 * fcap)

    halves, outgoing, heads = collect(info, row_list, out_list, m3, per, width)
    heads = [heads[0]] + [send(heads[x], "prow", flip(procs, x)) for x in range(1, procs)]
    bits = [1 << b for b in range(procs.bit_length() - 1)]
    turned = bits[len(bits) // 2 :] + bits[: len(bits) // 2]
    gathered = []
    for half, order in zip(halves, (bits, turned)):
        bufs, kinds = [half], [0]
        for bit in order:
            bufs = bufs + [send(buf, "prow", flip(procs, bit)) for buf in bufs]
            kinds = kinds + [kind ^ bit for kind in kinds]
        gathered.append((bufs, tuple(kinds)))
    displaced = [outgoing[0]] + [
        send(outgoing[x], "prow", [(s, s ^ x) for s in range(2)]) for x in range(1, procs)
    ]
    return info, src_owner, src_rank, heads, gathered, displaced, spots


def exchange_any(m3, width, info, src, dest):
    per = width // LANES
    half = m3.shape[1] // 2
    me = info[0]
    src_owner, src_local, _ = src
    dest_owner, dest_local, _ = dest
    rows = jnp.where((src_owner == me)[:, None, None], m3[src_local], 0.0)
    rows = lax.psum(rows.reshape(-1, LANES), "prow").reshape(rows.shape)
    displaced = []
    for source in range(2):
        top = jnp.where(me == source, m3[:width], 0.0)
        displaced.append(lax.psum(top.reshape(-1, LANES), "prow").reshape(top.shape))
    heads = [jnp.concatenate([rows[:, :per], top[:, :per]]) for top in displaced]
    gathered = [([rows[:, :half]], (0,)), ([rows[:, half:]], (0,))]
    spots = jnp.where(dest_owner == me, dest_local, -1)
    order = jnp.arange(2 * width, dtype=jnp.int32)
    first = jnp.concatenate([jnp.zeros((1,), jnp.int32), info[1:]])
    return first, jnp.zeros_like(order), order, heads, gathered, displaced, spots


def factor(cap, fcap, m3, inv, info, src, dest, out=None):
    rows, groups, _ = m3.shape
    width = inv.shape[1]
    chips = lax.axis_size("pcol") // 2
    per = width // LANES
    z = info[2]
    m2 = m3.reshape(rows * groups, LANES)
    m4 = m3.reshape(rows, groups // per, per, LANES)
    hop = [(q, q + 2) for q in range(2 * chips - 2)]
    swap = [(q, q ^ 1) for q in range(2 * chips)]

    chunk = rows // CHUNKS
    length = CHUNKS // CHAINS
    pieces = panel(m4, 0, CHAINS, chunk) + panel(m4, CHAINS, CHUNKS - CHAINS, chunk)
    own = [[] for _ in range(CHAINS)]
    sib = [[] for _ in range(CHAINS)]
    for t in range(length + chips - 1):
        for k in range(CHAINS):
            piece = pieces[t * CHAINS + k].reshape(chunk * per, LANES) if t < length else None
            if t == 0:
                cur = piece
            else:
                cur = send(own[k][-1], "pcol", hop)
                if t < length:
                    cur = jnp.where(z == 0, piece, cur)
            own[k].append(cur)
            sib[k].append(send(cur, "pcol", swap))

    if cap is None:
        cap, moves = 2 * width, exchange_any(m3, width, info, src, dest)
    else:
        moves = exchange(cap, fcap, m3, width, info, src, dest)
    seen, owner, rank, heads, gathered, displaced, spots = moves
    tab, ftab = tables(seen, owner, rank, heads, cap, width)

    def spread(table):
        table = table.reshape(-1, LANES)
        for h in range(1, chips):
            pairs = [(2 * h - 2, 2 * h), (2 * h - 1, 2 * h + 1)]
            table = jnp.where(z == h, lax.ppermute(table, "pcol", pairs), table)
        return table, lax.ppermute(table, "pcol", swap)

    tab_own, tab_sib = spread(tab)
    ftab_own, ftab_sib = spread(ftab)
    (a_bufs, order_a), (b_bufs, order_b) = gathered
    uhl, brow, u01 = solve(
        seen, owner, rank, a_bufs, b_bufs, order_a, order_b, tab_own, tab_sib, inv, groups, per
    )
    fixed = moved(seen, displaced, ftab_own, ftab_sib, inv, u01, uhl, per)

    if out is not None:
        out = out.reshape(m2.shape)
    for t in range(length):
        bufs = []
        for k in range(CHAINS):
            bufs += own[k][t : t + chips] + sib[k][t : t + chips]
        out = bulk(
            info, bufs, m2, inv, u01, uhl, out, t * CHAINS * chunk, CHAINS, chunk, groups, per
        )
    return place(info, spots, fixed, brow, out.reshape(rows, groups, LANES))


def shards(matrix, pivots, inverse_blocks):
    row_blocks, _, width, blocks, _, _ = matrix.shape
    procs = lax.axis_size("prow")
    me = lax.axis_index("prow").astype(jnp.int32)
    mc = lax.axis_index("pcol").astype(jnp.int32)
    info = jnp.stack([me, mc, mc // 2, mc % 2])
    so, sl, sr, do, dl, dr, src_most, dest_most = plan(pivots, width, procs, me)
    mean = 2 * width // procs
    cap = min(2 * width, (mean + 3 * mean // 8 + 7) // 8 * 8)
    fmean = width // procs
    fcap = min(width, (fmean + fmean // 2 + 7) // 8 * 8)
    again = (src_most > cap) | (dest_most > fcap)
    m3 = matrix.reshape(row_blocks * width, -1, LANES)
    args = (m3, inverse_blocks, info, (so, sl, sr), (do, dl, dr))
    out = factor(cap, fcap, *args)

    out = lax.cond(
        again,
        lambda done, *rest: factor(None, None, *rest, done),
        lambda done, *rest: done,
        out,
        *args,
    )
    return out.reshape(matrix.shape)


def solution(mesh):
    return jax.shard_map(
        shards,
        mesh=mesh,
        in_specs=(P(None, "prow", None, None, "pcol", None), P(), P()),
        out_specs=P(None, "prow", None, None, "pcol", None),
        check_vma=False,
    )
```

time: 725 us -> 310 us (0.43)
  Pallas kernels: 561 us -> 137 us
  starting transfers between devices: 57.6 us -> 101 us
  waiting for transfers between devices: 57.2 us -> 27.8 us
  loops' own time: 9.85 us -> 1.24 us
    pallas_call x23 -> x15, Pallas kernels: 561 us -> 137 us  [the longest x8 89.3 us: bulk(): pl.pallas_call(make_bulk_kernel(chips, count, chunk, tile, groups, per),...]
    ppermute x24 -> x54, starting transfers between devices: 48.1 us -> 93.8 us  [send(): return lax.ppermute(flat, axis, pairs).reshape(value.shape)]
    ppermute x24 -> x54, waiting for transfers between devices: 57.2 us -> 21.5 us  [send(): return lax.ppermute(flat, axis, pairs).reshape(value.shape)]
    cond x102 -> x0, local copies, waits for them, and re-layouts: 10.5 us -> none
    another operation x1, loops' own time: 9.85 us -> 1.24 us  [shards(): lax.cond(again, lambda done, *rest: factor(None, None, *rest, done), lamb...]
  transfers between devices with their start and end apart: 33 -> 62, of which waited for: 6 -> 8; matrix products, arithmetic and copies ran while one was open for 1% -> 2% of each run, Pallas kernels for 57% -> 36%
where the time goes in v2:
time: 310 us; the launch traced here: 305 us
  Pallas kernels  137 us (44%)
  starting transfers between devices  101 us (33%)
  waiting for transfers between devices  27.8 us (9%)
  between operations  17.1 us (6%)
  other arithmetic  12.7 us (4%)
  local copies, waits for them, and re-layouts  8.06 us (3%)
    ppermute x54, starting transfers between devices, send(): return lax.ppermute(flat, axis, pairs).reshape(value.shape)  93.8 us
    pallas_call x8, Pallas kernels, bulk(): pl.pallas_call(make_bulk_kernel(chips, count, chunk, tile, groups, per),...  89.3 us
    ppermute x54, waiting for transfers between devices, send(): return lax.ppermute(flat, axis, pairs).reshape(value.shape)  21.5 us
    pallas_call x1, Pallas kernels, solve(): pl.pallas_call(functools.partial(solve_kernel, procs, order_a, order_b, g...  14.6 us
    pallas_call x1, Pallas kernels, moved(): pl.pallas_call(functools.partial(moved_kernel, len(bufs), groups, per), i...  8.32 us
    pallas_call x1, Pallas kernels, collect(): pl.pallas_call(functools.partial(collect_kernel, procs, per), in_specs=[S...  8.09 us
    pallas_call x1, Pallas kernels, place(): pl.pallas_call(place_kernel, in_specs=[SMEM, SMEM, VMEM, VMEM, ANY], out_...  6.75 us
    unnamed x180, local copies, waits for them, and re-layouts  6.66 us
  transfers between devices with their start and end apart: 62, of which 8 were waited for; matrix products, arithmetic and copies ran while one was open for 2% of the time, Pallas kernels for 36%

profile of v2, /device:TPU:0, one launch (start us, length us, event | category | flops | bytes accessed | tf_op | source)
XLA Modules:
  0.0 304.6 jit_solution(5704735709032487036)
XLA Ops:
  13.9 8.1 %collect.1 = (f32[176,8,128]{2,1,0:T(8,128)}, f32[176,8,128]{2,1,0:T(8,128)}, f32[96,16,128]{2,1,0:T(8,128)}, f32[96,16,128]{2,1,0:T(8,128)}, f32[96,16,128]{2,1...) custom-call(s32[4]{0:T(128)S(1)} %pad_add_fusion.6.info_ref, ...), custom_call_target="tpu_custom_call" | custom-call | bytes 18350080 | tf_op jit(solution)/shard_map/collect/pallas_call | solution.py:161
  38.4 4.2 %panel.6 = (f32[256,2,128]{2,1,0:T(2,128)}, f32[256,2,128]{2,1,0:T(2,128)}, f32[256,2,128]{2,1,0:T(2,128)}, f32[256,2,128]{2,1,0:T(2,128)}, f32[256,2,128]{2,1,0...) custom-call(f32[4096,8,2,128]{3,2,1,0:T(2,128)} %bitcast.81), custom_call_target="tpu_custom_call" | custom-call | bytes 7340032 | tf_op jit(solution)/shard_map/panel/pallas_call | solution.py:100
  49.4 4.1 %tables.3 = (f32[256,2,128]{2,1,0:T(2,128)}, f32[192,2,128]{2,1,0:T(2,128)}) custom-call(s32[4]{0:T(128)S(1)} %pad_add_fusion.6.info_ref, s32[512]{0:T(512)S(1)} %get-tuple-element.312.owner_ref, s32[512]{0:T(512)} %copy-done.123, f32[272,2,128]{2,1,0:T(2,128)} %get-tuple-element.100.rest_0_, f32[272,2,128]{2,1,0:T(2,128)} %bitcast.112, ...), custom_call_target="tpu_custom_call" | custom-call | bytes 2228224 | tf_op jit(solution)/shard_map/tables/pallas_call | solution.py:210
  60.0 4.3 %collective-permute-start.85 = (f32[512,128]{1,0:T(8,128)S(1)}, f32[512,128]{1,0:T(8,128)S(1)}, u32[]{:S(2)}, u32[]{:S(2)}) collective-permute-start(f32[512,128]{1,0:T(8,128)S(1)} %broadcast_select_fusion.26.rest_9_.rest_8_), channel_id=1, source_target_pairs={{0,2},{1,3},{2,4},{3,5},{4,6},{5,7},{8,10},{9,11},{10,12},{11,13},... | collective-permute-start | bytes 786440 | tf_op jit(solution)/shard_map/ppermute | solution.py:531
  74.6 4.3 %collective-permute-start.72 = (f32[512,128]{1,0:T(8,128)S(1)}, f32[512,128]{1,0:T(8,128)S(1)}, u32[]{:S(2)}, u32[]{:S(2)}) collective-permute-start(f32[512,128]{1,0:T(8,128)S(1)} %broadcast_select_fusion.32.rest_2_.rest_1_.rest_0_), channel_id=1, source_target_pairs={{0,2},{1,3},{2,4},{3,5},{4,6},{5,7},{8,10},{9,11},{10,12},{11,13},... | collective-permute-start | bytes 786440 | tf_op jit(solution)/shard_map/ppermute | solution.py:531
  81.3 4.1 %collective-permute-done.72 = f32[512,128]{1,0:T(8,128)S(1)} collective-permute-done((f32[512,128]{1,0:T(8,128)S(1)}, f32[512,128]{1,0:T(8,128)S(1)}, u32[]{:S(2)}, u32[]{:S(2)}) %collective-permute-start.72) | collective-permute-done | bytes 262176 | tf_op jit(solution)/shard_map/ppermute | solution.py:531
  89.3 7.4 %collective-permute-start.73 = (f32[512,128]{1,0:T(8,128)S(1)}, f32[512,128]{1,0:T(8,128)S(1)}, u32[]{:S(2)}, u32[]{:S(2)}) collective-permute-start(f32[512,128]{1,0:T(8,128)S(1)} %broadcast_select_fusion.31.rest_3_.rest_2_.rest_1_.rest_0_), channel_id=1, source_target_pairs={{0,2},{1,3},{2,4},{3,5},{4,6},{5,7},{8,10},{9,11},{10,12},{11,13},... | collective-permute-start | bytes 786440 | tf_op jit(solution)/shard_map/ppermute | solution.py:531
  100.3 4.4 %collective-permute-start.87 = (f32[512,128]{1,0:T(8,128)S(1)}, f32[512,128]{1,0:T(8,128)S(1)}, u32[]{:S(2)}, u32[]{:S(2)}) collective-permute-start(f32[512,128]{1,0:T(8,128)S(1)} %broadcast_select_fusion.24.rest_11_.rest_10_.rest_9_.rest_8_), channel_id=1, source_target_pairs={{0,2},{1,3},{2,4},{3,5},{4,6},{5,7},{8,10},{9,11},{10,12},{11,13},... | collective-permute-start | bytes 786440 | tf_op jit(solution)/shard_map/ppermute | solution.py:531
  108.5 4.4 %collective-permute-start.74 = (f32[512,128]{1,0:T(8,128)S(1)}, f32[512,128]{1,0:T(8,128)S(1)}, u32[]{:S(2)}, u32[]{:S(2)}) collective-permute-start(f32[512,128]{1,0:T(8,128)S(1)} %broadcast_select_fusion.30.rest_3_.rest_2_.rest_1_.rest_0_), channel_id=1, source_target_pairs={{0,2},{1,3},{2,4},{3,5},{4,6},{5,7},{8,10},{9,11},{10,12},{11,13},... | collective-permute-start | bytes 786440 | tf_op jit(solution)/shard_map/ppermute | solution.py:531
  119.9 5.1 %collective-permute-start.88 = (f32[512,128]{1,0:T(8,128)S(1)}, f32[512,128]{1,0:T(8,128)S(1)}, u32[]{:S(2)}, u32[]{:S(2)}) collective-permute-start(f32[512,128]{1,0:T(8,128)S(1)} %broadcast_select_fusion.23.rest_11_.rest_10_.rest_9_.rest_8_), channel_id=1, source_target_pairs={{0,2},{1,3},{2,4},{3,5},{4,6},{5,7},{8,10},{9,11},{10,12},{11,13},... | collective-permute-start | bytes 786440 | tf_op jit(solution)/shard_map/ppermute | solution.py:531
  125.8 4.8 %collective-permute-done.88 = f32[512,128]{1,0:T(8,128)S(1)} collective-permute-done((f32[512,128]{1,0:T(8,128)S(1)}, f32[512,128]{1,0:T(8,128)S(1)}, u32[]{:S(2)}, u32[]{:S(2)}) %collective-permute-start.88) | collective-permute-done | bytes 262176 | tf_op jit(solution)/shard_map/ppermute | solution.py:531
  135.4 3.7 %collective-permute-start.51 = (f32[1536,128]{1,0:T(8,128)}, f32[1536,128]{1,0:T(8,128)S(1)}, u32[]{:S(2)}, u32[]{:S(2)}) collective-permute-start(f32[1536,128]{1,0:T(8,128)} %bitcast.38), channel_id=1, source_target_pairs={{0,16},{8,24},{1,17},{9,25},{2,18},{10,26},{3,19},{11,27},{4,20},{... | collective-permute-start | bytes 2359304 | tf_op jit(solution)/shard_map/ppermute | solution.py:531
  141.7 14.6 %solve.3 = (bf16[2,512,2048]{2,1,0:T(8,128)(2,1)}, f32[512,16,128]{2,1,0:T(8,128)}, f32[256,256]{1,0:T(8,128)}) custom-call(s32[4]{0:T(128)} %copy-done.114, s32[512]{0:T(512)} %copy-done.117, s32[512]{0:T(512)} %copy-done.123, f32[176,8,128]{2,1,0:T(8,128)} %get-tuple-element.105.rest_0_, f32[176,8,128]{2,1,0:T(8,128)} %bitcast.169, ...), custom_call_target="tpu_custom_call" | custom-call | flops 2415919104 | bytes 12582912 | tf_op jit(solution)/shard_map/solve/pallas_call | solution.py:294
  157.2 11.2 %bulk.24.rest_20_ = f32[65536,128]{1,0:T(8,128)} custom-call(s32[4]{0:T(128)S(1)} %copy-done.115, f32[512,128]{1,0:T(8,128)} %bitcast.116, f32[512,128]{1,0:T(8,128)} %copy-done.59, f32[512,128]{1,0:T(8,128)} %copy-done.42, f32[512,128]{1,0:T(8,128)} %copy-done.3, f32[512,128]{1,0:T(8,128)} %collective-permute-done.110.rest_4_, f32[512,128]{1,0:T(8,128)} %copy-done.64, ...), custom_call_target="tpu_custom_call" | custom-call | flops 3221225472 | bytes 8388608 | tf_op jit(solution)/shard_map/bulk/pallas_call | solution.py:375
  169.0 5.0 %collective-permute-start.75 = (f32[512,128]{1,0:T(8,128)S(1)}, f32[512,128]{1,0:T(8,128)S(1)}, u32[]{:S(2)}, u32[]{:S(2)}) collective-permute-start(f32[512,128]{1,0:T(8,128)S(1)} %broadcast_select_fusion.29.rest_3_.rest_2_.rest_1_.rest_0_), channel_id=1, source_target_pairs={{0,2},{1,3},{2,4},{3,5},{4,6},{5,7},{8,10},{9,11},{10,12},{11,13},... | collective-permute-start | bytes 786440 | tf_op jit(solution)/shard_map/ppermute | solution.py:531
  174.1 11.2 %bulk.25.rest_20_ = f32[65536,128]{1,0:T(8,128)} custom-call(s32[4]{0:T(128)S(1)} %copy-done.115, f32[512,128]{1,0:T(8,128)} %copy-done.59, f32[512,128]{1,0:T(8,128)} %copy-done.42, f32[512,128]{1,0:T(8,128)} %copy-done.3, f32[512,128]{1,0:T(8,128)} %copy-done.13, f32[512,128]{1,0:T(8,128)} %copy-done.64, ...), custom_call_target="tpu_custom_call", output_to_operand_aliasing={{}: (21, {})} | custom-call | flops 3221225472 | bytes 8388608 | tf_op jit(solution)/shard_map/bulk/pallas_call | solution.py:375
  188.5 8.3 %moved.3.f_ref = f32[192,16,128]{2,1,0:T(8,128)} custom-call(s32[4]{0:T(128)S(1)} %copy-done.115, f32[96,16,128]{2,1,0:T(8,128)} %get-tuple-element.96.rest_0_, f32[96,16,128]{2,1,0:T(8,128)} %bitcast.107, f32[96,16,128]{2,1,0:T(8,128)} %bitcast.108, f32[96,16,128]{2,1,0:T(8,128)} %bitcast.109, f32[384,128]{1,0:T(8,128)} %copy-done.78, ...), custom_call_target="tpu_custom_call" | custom-call | flops 1207959552 | bytes 3145728 | tf_op jit(solution)/shard_map/moved/pallas_call | solution.py:425
  202.7 11.2 %bulk.26.rest_20_ = f32[65536,128]{1,0:T(8,128)} custom-call(s32[4]{0:T(128)S(1)} %copy-done.115, f32[512,128]{1,0:T(8,128)} %copy-done.42, f32[512,128]{1,0:T(8,128)} %copy-done.3, f32[512,128]{1,0:T(8,128)} %copy-done.13, f32[512,128]{1,0:T(8,128)} %copy-done.15, f32[512,128]{1,0:T(8,128)} %copy-done.46, ...), custom_call_target="tpu_custom_call", output_to_operand_aliasing={{}: (21, {})} | custom-call | flops 3221225472 | bytes 8388608 | tf_op jit(solution)/shard_map/bulk/pallas_call | solution.py:375
  219.3 11.2 %bulk.27.rest_20_ = f32[65536,128]{1,0:T(8,128)} custom-call(s32[4]{0:T(128)S(1)} %copy-done.115, f32[512,128]{1,0:T(8,128)} %copy-done.3, f32[512,128]{1,0:T(8,128)} %copy-done.13, f32[512,128]{1,0:T(8,128)} %copy-done.15, f32[512,128]{1,0:T(8,128)} %copy-done.17, f32[512,128]{1,0:T(8,128)} %copy-done.22, ...), custom_call_target="tpu_custom_call", output_to_operand_aliasing={{}: (21, {})} | custom-call | flops 3221225472 | bytes 8388608 | tf_op jit(solution)/shard_map/bulk/pallas_call | solution.py:375
  235.7 11.2 %bulk.28.rest_20_ = f32[65536,128]{1,0:T(8,128)} custom-call(s32[4]{0:T(128)S(1)} %copy-done.115, f32[512,128]{1,0:T(8,128)} %copy-done.13, f32[512,128]{1,0:T(8,128)} %copy-done.15, f32[512,128]{1,0:T(8,128)} %copy-done.17, f32[512,128]{1,0:T(8,128)} %copy-done.19, f32[512,128]{1,0:T(8,128)} %copy-done.24, ...), custom_call_target="tpu_custom_call", output_to_operand_aliasing={{}: (21, {})} | custom-call | flops 3221225472 | bytes 8388608 | tf_op jit(solution)/shard_map/bulk/pallas_call | solution.py:375
  252.3 11.2 %bulk.29.rest_20_ = f32[65536,128]{1,0:T(8,128)} custom-call(s32[4]{0:T(128)S(1)} %copy-done.115, f32[512,128]{1,0:T(8,128)} %copy-done.15, f32[512,128]{1,0:T(8,128)} %copy-done.17, f32[512,128]{1,0:T(8,128)} %copy-done.19, f32[512,128]{1,0:T(8,128)} %copy-done.50, f32[512,128]{1,0:T(8,128)} %copy-done.27, ...), custom_call_target="tpu_custom_call", output_to_operand_aliasing={{}: (21, {})} | custom-call | flops 3221225472 | bytes 8388608 | tf_op jit(solution)/shard_map/bulk/pallas_call | solution.py:375
  265.5 11.2 %bulk.30.rest_20_ = f32[65536,128]{1,0:T(8,128)} custom-call(s32[4]{0:T(128)S(1)} %copy-done.115, f32[512,128]{1,0:T(8,128)} %copy-done.17, f32[512,128]{1,0:T(8,128)} %copy-done.19, f32[512,128]{1,0:T(8,128)} %copy-done.50, f32[512,128]{1,0:T(8,128)} %copy-done.69, f32[512,128]{1,0:T(8,128)} %copy-done.33, ...), custom_call_target="tpu_custom_call", output_to_operand_aliasing={{}: (21, {})} | custom-call | flops 3221225472 | bytes 8388608 | tf_op jit(solution)/shard_map/bulk/pallas_call | solution.py:375
  278.1 11.2 %bulk.31 = f32[65536,128]{1,0:T(8,128)} custom-call(s32[4]{0:T(128)S(1)} %copy-done.115, f32[512,128]{1,0:T(8,128)} %copy-done.19, f32[512,128]{1,0:T(8,128)} %copy-done.50, f32[512,128]{1,0:T(8,128)} %copy-done.69, f32[512,128]{1,0:T(8,128)} %copy-done.89, f32[512,128]{1,0:T(8,128)} %copy-done.38, ...), custom_call_target="tpu_custom_call", output_to_operand_aliasing={{}: (21, {})} | custom-call | flops 3221225472 | bytes 8388608 | tf_op jit(solution)/shard_map/bulk/pallas_call | solution.py:375
  289.4 6.8 %place.3 = f32[4096,16,128]{2,1,0:T(8,128)} custom-call(s32[4]{0:T(128)S(1)} %copy-done.115, s32[192]{0:T(256)} %sub.61.spot_ref, f32[192,16,128]{2,1,0:T(8,128)} %moved.3.f_ref, f32[512,16,128]{2,1,0:T(8,128)} %get-tuple-element.110.brow_ref, f32[4096,16,128]{2,1,0:T(8,128)} %bitcast.103), custom_call_target="tpu_custom_call", output_to_operand_aliasing={{}: (4, {})} | custom-call | bytes 11534336 | tf_op jit(solution)/shard_map/place/pallas_call | solution.py:480
  (350 shorter events, 104.8 us)
Async XLA Ops:
  22.0 23.7 %collective-permute-start.53 = (f32[544,128]{1,0:T(8,128)}, f32[544,128]{1,0:T(8,128)S(1)}, u32[]{:S(2)}, u32[]{:S(2)}) collective-permute-start(f32[544,128]{1,0:T(8,128)} %bitcast.177), channel_id=1, source_target_pairs={{0,8},{8,0},{16,24},{24,16},{1,9},{9,1},{17,25},{25,17},{2,10},{10... | collective-permute-start | bytes 835592 | tf_op jit(solution)/shard_map/ppermute | solution.py:531
  25.5 20.7 %collective-permute-start.54 = (f32[544,128]{1,0:T(8,128)}, f32[544,128]{1,0:T(8,128)S(1)}, u32[]{:S(2)}, u32[]{:S(2)}) collective-permute-start(f32[544,128]{1,0:T(8,128)} %bitcast.176), channel_id=1, source_target_pairs={{0,16},{8,24},{16,0},{24,8},{1,17},{9,25},{17,1},{25,9},{2,18},{10... | collective-permute-start | bytes 835592 | tf_op jit(solution)/shard_map/ppermute | solution.py:531
  27.2 19.5 %collective-permute-start.55 = (f32[544,128]{1,0:T(8,128)}, f32[544,128]{1,0:T(8,128)S(1)}, u32[]{:S(2)}, u32[]{:S(2)}) collective-permute-start(f32[544,128]{1,0:T(8,128)} %bitcast.175), channel_id=1, source_target_pairs={{0,24},{8,16},{16,8},{24,0},{1,25},{9,17},{17,9},{25,1},{2,26},{10... | collective-permute-start | bytes 835592 | tf_op jit(solution)/shard_map/ppermute | solution.py:531
  34.0 19.5 %collective-permute-start.84 = (f32[512,128]{1,0:T(8,128)}, f32[512,128]{1,0:T(8,128)S(1)}, u32[]{:S(2)}, u32[]{:S(2)}) collective-permute-start(f32[512,128]{1,0:T(8,128)} %bitcast.118), channel_id=1, source_target_pairs={{0,2},{1,3},{2,4},{3,5},{4,6},{5,7},{8,10},{9,11},{10,12},{11,13},... | collective-permute-start | bytes 786440 | tf_op jit(solution)/shard_map/ppermute | solution.py:531
  44.6 36.7 %collective-permute-start.110 = (f32[512,128]{1,0:T(8,128)S(1)}, f32[512,128]{1,0:T(8,128)}, u32[]{:S(2)}, u32[]{:S(2)}) collective-permute-start(f32[512,128]{1,0:T(8,128)S(1)} %bitcast.117), channel_id=1, source_target_pairs={{0,1},{1,0},{2,3},{3,2},{4,5},{5,4},{6,7},{7,6},{8,9},{9,8},{10,11... | collective-permute-start | bytes 786440 | tf_op jit(solution)/shard_map/ppermute | solution.py:531
  45.7 40.5 %collective-permute-start.111 = (f32[512,128]{1,0:T(8,128)S(1)}, f32[512,128]{1,0:T(8,128)S(1)}, u32[]{:S(2)}, u32[]{:S(2)}) collective-permute-start(f32[512,128]{1,0:T(8,128)S(1)} %bitcast.120), channel_id=1, source_target_pairs={{0,1},{1,0},{2,3},{3,2},{4,5},{5,4},{6,7},{7,6},{8,9},{9,8},{10,11... | collective-permute-start | bytes 786440 | tf_op jit(solution)/shard_map/ppermute | solution.py:531
  46.2 52.4 %collective-permute-start.60 = (f32[1408,128]{1,0:T(8,128)}, f32[1408,128]{1,0:T(8,128)S(1)}, u32[]{:S(2)}, u32[]{:S(2)}) collective-permute-start(f32[1408,128]{1,0:T(8,128)} %bitcast.49), channel_id=1, source_target_pairs={{0,8},{8,0},{16,24},{24,16},{1,9},{9,1},{17,25},{25,17},{2,10},{10... | collective-permute-start | bytes 2162696 | tf_op jit(solution)/shard_map/ppermute | solution.py:531
  86.2 18.6 %collective-permute-start.63 = (f32[1408,128]{1,0:T(8,128)}, f32[1408,128]{1,0:T(8,128)S(1)}, u32[]{:S(2)}, u32[]{:S(2)}) collective-permute-start(f32[1408,128]{1,0:T(8,128)} %bitcast.53), channel_id=1, source_target_pairs={{0,16},{8,24},{16,0},{24,8},{1,17},{9,25},{17,1},{25,9},{2,18},{10... | collective-permute-start | bytes 2162696 | tf_op jit(solution)/shard_map/ppermute | solution.py:531
  96.7 19.9 %collective-permute-start.61 = (f32[1408,128]{1,0:T(8,128)}, f32[1408,128]{1,0:T(8,128)S(1)}, u32[]{:S(2)}, u32[]{:S(2)}) collective-permute-start(f32[1408,128]{1,0:T(8,128)} %bitcast.49), channel_id=1, source_target_pairs={{0,16},{8,24},{16,0},{24,8},{1,17},{9,25},{17,1},{25,9},{2,18},{10... | collective-permute-start | bytes 2162696 | tf_op jit(solution)/shard_map/ppermute | solution.py:531
  116.7 18.8 %collective-permute-start.62 = (f32[1408,128]{1,0:T(8,128)}, f32[1408,128]{1,0:T(8,128)S(1)}, u32[]{:S(2)}, u32[]{:S(2)}) collective-permute-start(f32[1408,128]{1,0:T(8,128)} %copy-done.134), channel_id=1, source_target_pairs={{0,16},{8,24},{16,0},{24,8},{1,17},{9,25},{17,1},{25,9},{2,18},{10... | collective-permute-start | bytes 2162696 | tf_op jit(solution)/shard_map/ppermute | solution.py:531
  118.5 20.6 %collective-permute-start.65 = (f32[1408,128]{1,0:T(8,128)S(1)}, f32[1408,128]{1,0:T(8,128)S(1)}, u32[]{:S(2)}, u32[]{:S(2)}) collective-permute-start(f32[1408,128]{1,0:T(8,128)S(1)} %collective-permute-done.63), channel_id=1, source_target_pairs={{0,8},{8,0},{16,24},{24,16},{1,9},{9,1},{17,25},{25,17},{2,10},{10... | collective-permute-start | bytes 2162696 | tf_op jit(solution)/shard_map/ppermute | solution.py:531
  125.2 31.2 %collective-permute-start.104 = (f32[512,128]{1,0:T(8,128)S(1)}, f32[512,128]{1,0:T(8,128)S(1)}, u32[]{:S(2)}, u32[]{:S(2)}) collective-permute-start(f32[512,128]{1,0:T(8,128)S(1)} %broadcast_select_fusion.31.rest_3_.rest_2_.rest_1_.rest_0_), channel_id=1, source_target_pairs={{0,1},{1,0},{2,3},{3,2},{4,5},{5,4},{6,7},{7,6},{8,9},{9,8},{10,11... | collective-permute-start | bytes 786440 | tf_op jit(solution)/shard_map/ppermute | solution.py:531
  130.6 25.9 %collective-permute-start.105 = (f32[512,128]{1,0:T(8,128)S(1)}, f32[512,128]{1,0:T(8,128)S(1)}, u32[]{:S(2)}, u32[]{:S(2)}) collective-permute-start(f32[512,128]{1,0:T(8,128)S(1)} %broadcast_select_fusion.24.rest_11_.rest_10_.rest_9_.rest_8_), channel_id=1, source_target_pairs={{0,1},{1,0},{2,3},{3,2},{4,5},{5,4},{6,7},{7,6},{8,9},{9,8},{10,11... | collective-permute-start | bytes 786440 | tf_op jit(solution)/shard_map/ppermute | solution.py:531
  130.7 54.6 %collective-permute-start.50 = (f32[1536,128]{1,0:T(8,128)}, f32[1536,128]{1,0:T(8,128)S(1)}, u32[]{:S(2)}, u32[]{:S(2)}) collective-permute-start(f32[1536,128]{1,0:T(8,128)} %bitcast.36), channel_id=1, source_target_pairs={{0,8},{8,0},{1,9},{9,1},{2,10},{10,2},{3,11},{11,3},{4,12},{12,4},... | collective-permute-start | bytes 2359304 | tf_op jit(solution)/shard_map/ppermute | solution.py:531
  135.4 49.9 %collective-permute-start.51 = (f32[1536,128]{1,0:T(8,128)}, f32[1536,128]{1,0:T(8,128)S(1)}, u32[]{:S(2)}, u32[]{:S(2)}) collective-permute-start(f32[1536,128]{1,0:T(8,128)} %bitcast.38), channel_id=1, source_target_pairs={{0,16},{8,24},{1,17},{9,25},{2,18},{10,26},{3,19},{11,27},{4,20},{... | collective-permute-start | bytes 2359304 | tf_op jit(solution)/shard_map/ppermute | solution.py:531
  139.2 46.7 %collective-permute-start.52 = (f32[1536,128]{1,0:T(8,128)}, f32[1536,128]{1,0:T(8,128)S(1)}, u32[]{:S(2)}, u32[]{:S(2)}) collective-permute-start(f32[1536,128]{1,0:T(8,128)} %bitcast.40), channel_id=1, source_target_pairs={{0,24},{8,16},{1,25},{9,17},{2,26},{10,18},{3,27},{11,19},{4,28},{... | collective-permute-start | bytes 2359304 | tf_op jit(solution)/shard_map/ppermute | solution.py:531
  168.4 19.4 %collective-permute-start.59 = (f32[384,128]{1,0:T(8,128)S(1)}, f32[384,128]{1,0:T(8,128)S(1)}, u32[]{:S(2)}, u32[]{:S(2)}) collective-permute-start(f32[384,128]{1,0:T(8,128)S(1)} %broadcast_select_fusion.39.rest_4_), channel_id=1, source_target_pairs={{0,1},{1,0},{2,3},{3,2},{4,5},{5,4},{6,7},{7,6},{8,9},{9,8},{10,11... | collective-permute-start | bytes 589832 | tf_op jit(solution)/shard_map/ppermute | solution.py:637
  169.0 27.9 %collective-permute-start.75 = (f32[512,128]{1,0:T(8,128)S(1)}, f32[512,128]{1,0:T(8,128)S(1)}, u32[]{:S(2)}, u32[]{:S(2)}) collective-permute-start(f32[512,128]{1,0:T(8,128)S(1)} %broadcast_select_fusion.29.rest_3_.rest_2_.rest_1_.rest_0_), channel_id=1, source_target_pairs={{0,2},{1,3},{2,4},{3,5},{4,6},{5,7},{8,10},{9,11},{10,12},{11,13},... | collective-permute-start | bytes 786440 | tf_op jit(solution)/shard_map/ppermute | solution.py:531
  196.9 19.5 %collective-permute-start.98 = (f32[512,128]{1,0:T(8,128)S(1)}, f32[512,128]{1,0:T(8,128)S(1)}, u32[]{:S(2)}, u32[]{:S(2)}) collective-permute-start(f32[512,128]{1,0:T(8,128)S(1)} %broadcast_select_fusion.28.rest_3_.rest_2_.rest_1_.rest_0_), channel_id=1, source_target_pairs={{0,1},{1,0},{2,3},{3,2},{4,5},{5,4},{6,7},{7,6},{8,9},{9,8},{10,11... | collective-permute-start | bytes 786440 | tf_op jit(solution)/shard_map/ppermute | solution.py:531
  199.1 19.5 %collective-permute-start.99 = (f32[512,128]{1,0:T(8,128)S(1)}, f32[512,128]{1,0:T(8,128)S(1)}, u32[]{:S(2)}, u32[]{:S(2)}) collective-permute-start(f32[512,128]{1,0:T(8,128)S(1)} %broadcast_select_fusion.21.rest_11_.rest_10_.rest_9_.rest_8_), channel_id=1, source_target_pairs={{0,1},{1,0},{2,3},{3,2},{4,5},{5,4},{6,7},{7,6},{8,9},{9,8},{10,11... | collective-permute-start | bytes 786440 | tf_op jit(solution)/shard_map/ppermute | solution.py:531
  214.0 18.8 %collective-permute-start.80 = (f32[512,128]{1,0:T(8,128)S(1)}, f32[512,128]{1,0:T(8,128)S(1)}, u32[]{:S(2)}, u32[]{:S(2)}) collective-permute-start(f32[512,128]{1,0:T(8,128)S(1)} %broadcast_select_fusion.27.rest_3_.rest_2_.rest_1_.rest_0_), channel_id=1, source_target_pairs={{0,1},{1,0},{2,3},{3,2},{4,5},{5,4},{6,7},{7,6},{8,9},{9,8},{10,11... | collective-permute-start | bytes 786440 | tf_op jit(solution)/shard_map/ppermute | solution.py:531
  216.3 18.7 %collective-permute-start.94 = (f32[512,128]{1,0:T(8,128)S(1)}, f32[512,128]{1,0:T(8,128)S(1)}, u32[]{:S(2)}, u32[]{:S(2)}) collective-permute-start(f32[512,128]{1,0:T(8,128)S(1)} %broadcast_select_fusion.20.rest_11_.rest_10_.rest_9_.rest_8_), channel_id=1, source_target_pairs={{0,1},{1,0},{2,3},{3,2},{4,5},{5,4},{6,7},{7,6},{8,9},{9,8},{10,11... | collective-permute-start | bytes 786440 | tf_op jit(solution)/shard_map/ppermute | solution.py:531
  230.5 18.8 %collective-permute-start.81 = (f32[512,128]{1,0:T(8,128)S(1)}, f32[512,128]{1,0:T(8,128)S(1)}, u32[]{:S(2)}, u32[]{:S(2)}) collective-permute-start(f32[512,128]{1,0:T(8,128)S(1)} %collective-permute-done.77.rest_3_.rest_2_.rest_1_), channel_id=1, source_target_pairs={{0,1},{1,0},{2,3},{3,2},{4,5},{5,4},{6,7},{7,6},{8,9},{9,8},{10,11... | collective-permute-start | bytes 786440 | tf_op jit(solution)/shard_map/ppermute | solution.py:531
  232.7 18.9 %collective-permute-start.95 = (f32[512,128]{1,0:T(8,128)S(1)}, f32[512,128]{1,0:T(8,128)S(1)}, u32[]{:S(2)}, u32[]{:S(2)}) collective-permute-start(f32[512,128]{1,0:T(8,128)S(1)} %collective-permute-done.91.rest_11_.rest_10_.rest_9_), channel_id=1, source_target_pairs={{0,1},{1,0},{2,3},{3,2},{4,5},{5,4},{6,7},{7,6},{8,9},{9,8},{10,11... | collective-permute-start | bytes 786440 | tf_op jit(solution)/shard_map/ppermute | solution.py:531
  (128 other events, 2368.7 us)
